TPU v7x, 512 devices: a whole 4x4x16 slice. The times are simulated.
512 devices in a mesh: ctx: 8 (over x, core), tab: 64 (over z, y).
Axes of the slice: x: 4, y: 4, z: 16, core: 2. Of those that a mesh axis runs over, the one named last changes fastest.
Arguments:
- item_owner: int32 [64, 1024, 1], P('tab', 'ctx'), may hold values from 0 to 63; in each aligned block of 128 rows (0 to 127, 128 to 255, ..., all dimensions but the last counted through in order) at most 4 rows name the same one
- item_row: int32 [64, 1024], P('tab', 'ctx'), may hold values from 0 to 63
- action_id: int32 [64, 1024], P('tab', 'ctx'), may hold values from 0 to 7
- history_len: int32 [64, 4], P('tab'), may hold values from 1 to 512, 1024 in all within a row
- masters: float32 [4096, 1024], P('tab'), may hold values from -6 to 6
- row_accum: float32 [4096], P('tab'), may hold values from 0.05 to 1
- action_table: float32 [8, 1024], replicated, may hold values from -3 to 3
- norm_gain: float32 [1024], replicated, may hold values from 0.1 to 1.9
- w_qkv: bfloat16 [1024, 1536], replicated, may hold values from -0.1875 to 0.1875
- d_attended: bfloat16 [64, 1024, 512], P('tab', 'ctx'), may hold values from -6 to 6
Outputs:
- attended: bfloat16 [64, 1024, 512], P('tab', 'ctx')
- row_grads: float32 [4096, 1024], P('tab')
- new_masters: float32 [4096, 1024], P('tab')
- new_accum: float32 [4096], P('tab')
Inputs may be any that keep to these rules, and one draw needn't show every extreme that they name: `item_owner`: among the 128 events of one device (aligned blocks of 128 events of a pack) at most 4 name the same shard, a bound that some block reaches. `history_len`: the 4 lengths of a pack sum to 1024; the longest is 512.
All inputs are finite; a program needn't handle non-finite values.
Results may differ from a plain program's by a relative error of at most 0.018.
Values may be sent and summed in bfloat16 or wider, within the bound.
A program may use at most 64 MiB of HBM per device.

v0:
```python
import math

import jax
import jax.numpy as jnp
from jax import lax
from jax.sharding import PartitionSpec as P

HEADS = 4


NORM_EPS = 1e-05
LEARN_RATE = 0.1


def passed_along(value, axis, by):
    size = lax.axis_size(axis)
    pairs = [(i, i + by) for i in range(size) if 0 <= i + by < size]
    return lax.ppermute(value, axis, pairs)


def silu_grad(argument):
    sigmoid_value = jax.nn.sigmoid(argument)
    return sigmoid_value * (1.0 + argument * (1.0 - sigmoid_value))


def segments_of(positions, user_ends):
    return jnp.sum((positions[:, None] >= user_ends[None, :]).astype(jnp.int32), axis=1)


def length_of(segment, lengths):
    choose = segment[:, None] == jnp.arange(lengths.shape[0], dtype=jnp.int32)[None, :]
    return jnp.sum(jnp.where(choose, lengths[None, :], 0), axis=1).astype(jnp.float32)


def split_block(block, head_count, head_dim):
    events = block.shape[0]
    attn_width = head_count * head_dim
    key_part = block[:, :attn_width].reshape(events, head_count, head_dim)
    values = block[:, attn_width:].reshape(events, head_count, head_dim)
    return (key_part, values)


def tile_weights(queries, key_part, allowed, query_len, score_scale):
    raw_scores = (
        jnp.einsum("qhd,khd->hqk", queries, key_part, preferred_element_type=jnp.float32)
        * score_scale
    )
    weights = jnp.where(
        allowed[None], jax.nn.silu(raw_scores) / query_len[None, :, None], 0.0
    ).astype(jnp.bfloat16)
    return (raw_scores, weights)


def forward_tile(summed_out, queries, block, allowed, query_len, score_scale):
    key_part, values = split_block(block, queries.shape[1], queries.shape[2])
    raw_scores, weights = tile_weights(queries, key_part, allowed, query_len, score_scale)
    return summed_out + jnp.einsum(
        "hqk,khd->qhd", weights, values, preferred_element_type=jnp.float32
    )


def tile_grads(queries, grad_out, block, allowed, query_len, score_scale):
    key_part, values = split_block(block, queries.shape[1], queries.shape[2])
    raw_scores, weights = tile_weights(queries, key_part, allowed, query_len, score_scale)
    grad_weights = jnp.einsum("qhd,khd->hqk", grad_out, values, preferred_element_type=jnp.float32)
    grad_raw = jnp.where(
        allowed[None],
        grad_weights * silu_grad(raw_scores) * score_scale / query_len[None, :, None],
        0.0,
    ).astype(jnp.bfloat16)
    return (key_part, weights, grad_raw)


def backward_tile(carry_pair, queries, grad_out, block, allowed, query_len, score_scale):
    grad_query, carried = carry_pair
    events = block.shape[0]
    key_part, weights, grad_raw = tile_grads(
        queries, grad_out, block, allowed, query_len, score_scale
    )
    grad_query = grad_query + jnp.einsum(
        "hqk,khd->qhd", grad_raw, key_part, preferred_element_type=jnp.float32
    )
    grad_key = jnp.einsum(
        "hqk,qhd->khd", grad_raw, queries, preferred_element_type=jnp.float32
    ).reshape(events, -1)
    grad_value = jnp.einsum(
        "hqk,qhd->khd", weights, grad_out, preferred_element_type=jnp.float32
    ).reshape(events, -1)
    carried = carried + jnp.concatenate([grad_key, grad_value], axis=1)
    return (grad_query, carried)


def adagrad_rows(rows_now, accum_now, gradient):
    accum_next = accum_now + jnp.mean(gradient * gradient, axis=1)
    return (rows_now - LEARN_RATE * gradient * lax.rsqrt(accum_next)[:, None], accum_next)


def per_device(
    item_owner,
    item_row,
    action_id,
    history_len,
    masters,
    row_accum,
    action_table,
    norm_gain,
    w_qkv,
    d_attended,
):
    owner_ids = item_owner[0, :, 0]
    wanted = item_row[0]
    events = owner_ids.shape[0]
    tab_peers = lax.axis_size("tab")
    capacity = max(2, 2 * events // tab_peers)
    table_rows = masters.shape[0]
    model_width = masters.shape[1]
    attn_width = d_attended.shape[2]
    head_count = HEADS
    head_dim = attn_width // head_count
    score_scale = 1.0 / math.sqrt(head_dim)
    owner_hot = (owner_ids[:, None] == jnp.arange(tab_peers, dtype=jnp.int32)[None, :]).astype(
        jnp.int32
    )
    before = jnp.cumsum(owner_hot, axis=0) - owner_hot
    slot_rank = jnp.sum(before * owner_hot, axis=1)
    requests = jnp.zeros((tab_peers, capacity), jnp.int32).at[owner_ids, slot_rank].set(wanted)
    arrived = lax.all_to_all(requests, "tab", split_axis=0, concat_axis=0, tiled=True)
    served = masters[arrived].astype(jnp.bfloat16)
    returned = lax.all_to_all(served, "tab", split_axis=0, concat_axis=0, tiled=True)
    fetched = returned[owner_ids, slot_rank]
    action_kinds = action_table.shape[0]
    action_hot = (
        action_id[0][:, None] == jnp.arange(action_kinds, dtype=jnp.int32)[None, :]
    ).astype(jnp.float32)
    inputs = fetched.astype(jnp.float32) + jnp.dot(
        action_hot, action_table, precision=lax.Precision.HIGHEST
    )
    centre = inputs - jnp.mean(inputs, axis=1, keepdims=True)
    inv_std = lax.rsqrt(jnp.mean(centre * centre, axis=1, keepdims=True) + NORM_EPS)
    normed = centre * inv_std
    hnorm = (normed * norm_gain[None, :]).astype(jnp.bfloat16)
    project = jnp.dot(hnorm, w_qkv, preferred_element_type=jnp.float32)
    activated = jax.nn.silu(project).astype(jnp.bfloat16)
    queries = activated[:, :attn_width].reshape(events, head_count, head_dim)
    keyval = activated[:, attn_width:]
    lengths = history_len[0]
    user_ends = jnp.cumsum(lengths)
    my_block = lax.axis_index("ctx")
    blocks = lax.axis_size("ctx")
    local_pos = jnp.arange(events, dtype=jnp.int32)
    query_pos = my_block * events + local_pos
    query_seg = segments_of(query_pos, user_ends)
    query_len = length_of(query_seg, lengths)
    stored = []
    current = keyval
    for turn_index in range(blocks):
        stored.append(current)
        if turn_index + 1 < blocks:
            current = passed_along(current, "ctx", 1)

    def tile_info(key_block):
        key_pos = key_block * events + local_pos
        key_seg = segments_of(key_pos, user_ends)
        allowed = (
            (query_seg[:, None] == key_seg[None, :])
            & (key_pos[None, :] <= query_pos[:, None])
            & (key_block >= 0)
        )
        occupied = (key_block == my_block) | (key_block >= 0) & (key_block < my_block) & (
            key_seg[events - 1] == query_seg[0]
        )
        return (allowed, occupied)

    attended = jnp.zeros((events, head_count, head_dim), jnp.float32)
    for turn_index in range(blocks):
        key_block = my_block - turn_index
        allowed, occupied = tile_info(key_block)
        block = stored[turn_index]
        attended = forward_tile(attended, queries, block, allowed, query_len, score_scale)
    attended_out = attended.reshape(1, events, attn_width).astype(jnp.bfloat16)
    grad_out = d_attended[0].reshape(events, head_count, head_dim)
    grad_query = jnp.zeros((events, head_count, head_dim), jnp.float32)
    carried = jnp.zeros((events, 2 * attn_width), jnp.float32)
    for turn_index in range(blocks):
        key_block = my_block - (blocks - 1) + turn_index
        allowed, occupied = tile_info(key_block)
        block = stored[blocks - 1 - turn_index]
        grad_query, carried = backward_tile(
            (grad_query, carried), queries, grad_out, block, allowed, query_len, score_scale
        )
        if turn_index + 1 < blocks:
            carried = passed_along(carried.astype(jnp.bfloat16), "ctx", -1).astype(carried.dtype)
    grad_qkv = jnp.concatenate([grad_query.reshape(events, attn_width), carried], axis=1)
    grad_project = (grad_qkv * silu_grad(project)).astype(jnp.bfloat16)
    grad_hnorm = lax.dot_general(
        grad_project, w_qkv, (((1,), (1,)), ((), ())), preferred_element_type=jnp.float32
    )
    grad_hat = grad_hnorm * norm_gain[None, :]
    event_grad = inv_std * (
        grad_hat
        - jnp.mean(grad_hat, axis=1, keepdims=True)
        - normed * jnp.mean(grad_hat * normed, axis=1, keepdims=True)
    )
    outgoing = (
        jnp.zeros((tab_peers, capacity, model_width), jnp.float32)
        .at[owner_ids, slot_rank]
        .set(event_grad)
    )
    incoming = lax.all_to_all(
        outgoing.astype(jnp.bfloat16), "tab", split_axis=0, concat_axis=0, tiled=True
    ).astype(outgoing.dtype)
    row_hot = (
        arrived.reshape(-1)[:, None] == jnp.arange(table_rows, dtype=jnp.int32)[None, :]
    ).astype(jnp.float32)
    local_grad = lax.dot_general(
        row_hot,
        incoming.reshape(-1, model_width),
        (((0,), (0,)), ((), ())),
        precision=lax.Precision.HIGHEST,
        preferred_element_type=jnp.float32,
    )
    summed_rows = lax.psum(local_grad.astype(jnp.bfloat16), "ctx").astype(jnp.float32)
    new_masters, new_accum = adagrad_rows(masters, row_accum, summed_rows)
    return (attended_out, summed_rows, new_masters, new_accum)


def solution(mesh):
    in_specs = (
        P("tab", "ctx", None),
        P("tab", "ctx"),
        P("tab", "ctx"),
        P("tab", None),
        P("tab", None),
        P("tab"),
        P(),
        P(),
        P(),
        P("tab", "ctx", None),
    )
    out_specs = (P("tab", "ctx", None), P("tab", None), P("tab", None), P("tab"))
    return jax.shard_map(
        per_device, mesh=mesh, in_specs=in_specs, out_specs=out_specs, check_vma=False
    )
```

profile of v0, /device:TPU:1, one launch (start us, length us, event | category | flops | bytes accessed | tf_op | source)
XLA Modules:
  0.0 424.2 jit_solution(3315163803737888940)
XLA Ops:
  9.8 11.0 %scatter_fusion = s32[64,4]{0,1:T(4,128)S(1)} fusion(s32[64,4]{0,1:T(4,128)S(1)} %broadcast.854, s32[128]{0:T(128)S(1)} %get-tuple-element.34, s32[128]{0:T(128)} %bitcast.398), kind=kCustom, calls=%fused_computation.2 | custom fusion | bytes 2560 | tf_op jit(solution)/shard_map/scatter | solution.py:126
  20.8 32.5 %all_to_all.22 = s32[64,1,4]{2,1,0:T(1,128)S(1)} all-to-all(s32[64,1,4]{2,1,0:T(1,128)S(1)} %copy.287), channel_id=1, replica_groups=mesh['ctx'=8,'tab'=64] {'tab'}, dimensions={0} | all-to-all | bytes 2048 | tf_op jit(solution)/shard_map/all_to_all | solution.py:127
  54.1 1.9 gather_fusion
  56.0 2.0 reshape.1265
  58.0 5.5 %all-to-all-start.1 = ((bf16[64,4,1024]{2,1,0:T(4,128)(2,1)}), bf16[64,4,1024]{2,1,0:T(4,128)(2,1)}, u32[]{:S(2)}, u32[]{:S(2)}) async-start(bf16[64,4,1024]{2,1,0:T(4,128)(2,1)} %reshape.1265), calls=%async_computation.1 | async-start | bytes 1048576 | tf_op jit(solution)/shard_map/all_to_all | solution.py:129
  71.2 21.1 %all-to-all-done.1 = bf16[64,4,1024]{2,1,0:T(4,128)(2,1)} async-done(((bf16[64,4,1024]{2,1,0:T(4,128)(2,1)}), bf16[64,4,1024]{2,1,0:T(4,128)(2,1)}, u32[]{:S(2)}, u32[]{:S(2)}) %all-to-all-start.1) | async-done | bytes 524320 | tf_op jit(solution)/shard_map/all_to_all | solution.py:129
  92.2 3.0 gather_fusion.1
  97.0 2.2 multiply_convert_fusion
  101.7 7.9 %collective-permute-start = (bf16[128,1024]{1,0:T(8,128)(2,1)}, bf16[128,1024]{1,0:T(8,128)(2,1)}, u32[]{:S(2)}, u32[]{:S(2)}) collective-permute-start(bf16[128,1024]{1,0:T(8,128)(2,1)} %slice.101), channel_id=1, source_target_pairs={{0,64},{64,128},{128,192},{192,256},{256,320},{320,384},{384,448},... | collective-permute-start | bytes 786440 | tf_op jit(solution)/shard_map/ppermute | solution.py:18
  117.2 1.9 fusion.109
  124.9 1.9 collective-permute-start.1
  129.5 1.9 fusion.108
  137.2 3.5 collective-permute-start.2
  143.5 1.9 fusion.107
  151.2 3.4 collective-permute-start.3
  157.3 1.9 fusion.106
  162.6 3.4 collective-permute-start.4
  167.8 1.9 fusion.43
  172.8 4.1 collective-permute-start.5
  178.9 1.9 fusion.44
  183.8 4.3 %collective-permute-start.6 = (bf16[128,1024]{1,0:T(8,128)(2,1)}, bf16[128,1024]{1,0:T(8,128)(2,1)S(1)}, u32[]{:S(2)}, u32[]{:S(2)}) collective-permute-start(bf16[128,1024]{1,0:T(8,128)(2,1)} %copy-done.27), channel_id=1, source_target_pairs={{0,64},{64,128},{128,192},{192,256},{256,320},{320,384},{384,448},... | collective-permute-start | bytes 786440 | tf_op jit(solution)/shard_map/ppermute | solution.py:18
  190.0 1.9 fusion.45
  194.3 3.1 select_convert_fusion
  206.0 1.9 collective-permute-start.7
  216.9 1.9 collective-permute-start.8
  227.9 1.9 collective-permute-start.9
  237.0 1.9 fusion.50
  238.9 1.9 collective-permute-start.10
  240.8 1.9 fusion.105
  247.2 1.9 fusion.51
  249.1 1.9 collective-permute-start.11
  251.0 1.9 fusion.104
  257.1 1.9 fusion.52
  258.9 1.9 collective-permute-start.12
  260.9 1.9 fusion.103
  266.9 1.9 fusion.53
  268.8 1.9 collective-permute-start.13
  270.7 2.5 fusion.37
  279.8 2.7 fusion.100
  284.7 18.4 %scatter_fusion.1 = f32[64,4,1024]{2,1,0:T(4,128)} fusion(f32[64,4,1024]{2,1,0:T(4,128)} %broadcast_in_dim.146, s32[128]{0:T(128)S(1)} %get-tuple-element.34, f32[128,1024]{1,0:T(8,128)} %subtract_multiply_fusion), kind=kCustom, calls=%fused_computation.3 | custom fusion | bytes 1573888 | tf_op jit(solution)/shard_map/scatter | solution.py:207
  303.1 2.2 convert_element_type.226
  305.3 5.7 %all-to-all-start.2 = ((bf16[64,4,1024]{2,1,0:T(4,128)(2,1)}), bf16[64,4,1024]{2,1,0:T(4,128)(2,1)}, u32[]{:S(2)}, u32[]{:S(2)}) async-start(bf16[64,4,1024]{2,1,0:T(4,128)(2,1)} %convert_element_type.226), calls=%async_computation.2 | async-start | bytes 1048576 | tf_op jit(solution)/shard_map/all_to_all | solution.py:209
  311.6 2.1 reduce.3
  322.0 17.9 %all-to-all-done.2 = bf16[64,4,1024]{2,1,0:T(4,128)(2,1)} async-done(((bf16[64,4,1024]{2,1,0:T(4,128)(2,1)}), bf16[64,4,1024]{2,1,0:T(4,128)(2,1)}, u32[]{:S(2)}, u32[]{:S(2)}) %all-to-all-start.2) | async-done | bytes 524320 | tf_op jit(solution)/shard_map/all_to_all | solution.py:209
  339.9 2.0 reshape.1237
  341.8 2.0 convolution_convert_fusion
  343.9 1.9 fusion.38
  347.4 67.5 %all-reduce.2.cloned.1.call-done = bf16[64,1024]{1,0:T(8,128)(2,1)} async-done(((bf16[64,1024]{1,0:T(8,128)(2,1)}), bf16[64,1024]{1,0:T(8,128)(2,1)}) %all-reduce.2.cloned.1.call-update) | async-done | bytes 131088 | tf_op jit(solution)/shard_map/psum | solution.py:222
  (208 shorter events, 133.9 us)
Async XLA Ops:
  7.2 89.8 %copy-start = (bf16[1024,1536]{1,0:T(8,128)(2,1)S(1)}, bf16[1024,1536]{1,0:T(8,128)(2,1)}, u32[]{:S(2)}) copy-start(bf16[1024,1536]{1,0:T(8,128)(2,1)} %param.18) | copy-start | bytes 9437188
  7.2 46.9 %copy-start.1 = (f32[64,1024]{1,0:T(8,128)S(1)}, f32[64,1024]{1,0:T(8,128)}, u32[]{:S(2)}) copy-start(f32[64,1024]{1,0:T(8,128)} %param.14) | copy-start | bytes 786436
  54.1 9.5 %copy-start.40 = (s32[1,4]{1,0:T(1,128)S(1)}, s32[1,4]{1,0:T(1,128)}, u32[]{:S(2)}) copy-start(s32[1,4]{1,0:T(1,128)} %param.13) | copy-start | bytes 52
  54.1 13.4 %copy-start.29 = (bf16[1,128,512]{2,1,0:T(8,128)(2,1)S(1)}, bf16[1,128,512]{2,1,0:T(8,128)(2,1)}, u32[]{:S(2)}) copy-start(bf16[1,128,512]{2,1,0:T(8,128)(2,1)} %param.19) | copy-start | bytes 393220
  58.0 34.2 %all-to-all-start.1 = ((bf16[64,4,1024]{2,1,0:T(4,128)(2,1)}), bf16[64,4,1024]{2,1,0:T(4,128)(2,1)}, u32[]{:S(2)}, u32[]{:S(2)}) async-start(bf16[64,4,1024]{2,1,0:T(4,128)(2,1)} %reshape.1265), calls=%async_computation.1 | async-start | bytes 1048576 | tf_op jit(solution)/shard_map/all_to_all | solution.py:129
  64.3 1.9 copy-start.32
  64.3 1.9 copy-start.33
  64.3 2.6 copy-start.36
  64.3 2.6 copy-start.35
  64.4 2.6 copy-start.37
  96.7 2.5 copy-start.4
  97.0 15.5 %copy-start.41 = (f32[128]{0:T(128)S(1)}, f32[128]{0:T(128)}, u32[]{:S(2)}) copy-start(f32[128]{0:T(128)} %convert_element_type.186) | copy-start | bytes 1540
  101.7 17.3 %collective-permute-start = (bf16[128,1024]{1,0:T(8,128)(2,1)}, bf16[128,1024]{1,0:T(8,128)(2,1)}, u32[]{:S(2)}, u32[]{:S(2)}) collective-permute-start(bf16[128,1024]{1,0:T(8,128)(2,1)} %slice.101), channel_id=1, source_target_pairs={{0,64},{64,128},{128,192},{192,256},{256,320},{320,384},{384,448},... | collective-permute-start | bytes 786440 | tf_op jit(solution)/shard_map/ppermute | solution.py:18
  112.5 2.9 copy-start.20
  123.6 4.2 copy-start.21
  124.9 1.9 copy-start.15
  124.9 6.5 %collective-permute-start.1 = (bf16[128,1024]{1,0:T(8,128)(2,1)}, bf16[128,1024]{1,0:T(8,128)(2,1)}, u32[]{:S(2)}, u32[]{:S(2)}) collective-permute-start(bf16[128,1024]{1,0:T(8,128)(2,1)} %collective-permute-done), channel_id=1, source_target_pairs={{0,64},{64,128},{128,192},{192,256},{256,320},{320,384},{384,448},... | collective-permute-start | bytes 786440 | tf_op jit(solution)/shard_map/ppermute | solution.py:18
  135.9 5.8 %copy-start.22 = (f32[4,128,128]{2,1,0:T(8,128)}, f32[4,128,128]{2,1,0:T(8,128)S(1)}, u32[]{:S(2)}) copy-start(f32[4,128,128]{2,1,0:T(8,128)S(1)} %convolution_multiply_fusion.6) | copy-start | bytes 786436
  137.2 3.5 copy-start.16
  137.2 8.1 %collective-permute-start.2 = (bf16[128,1024]{1,0:T(8,128)(2,1)}, bf16[128,1024]{1,0:T(8,128)(2,1)}, u32[]{:S(2)}, u32[]{:S(2)}) collective-permute-start(bf16[128,1024]{1,0:T(8,128)(2,1)} %collective-permute-done.1), channel_id=1, source_target_pairs={{0,64},{64,128},{128,192},{192,256},{256,320},{320,384},{384,448},... | collective-permute-start | bytes 786440 | tf_op jit(solution)/shard_map/ppermute | solution.py:18
  149.8 5.7 %copy-start.23 = (f32[4,128,128]{2,1,0:T(8,128)}, f32[4,128,128]{2,1,0:T(8,128)S(1)}, u32[]{:S(2)}) copy-start(f32[4,128,128]{2,1,0:T(8,128)S(1)} %convolution_multiply_fusion.5) | copy-start | bytes 786436
  151.2 3.4 copy-start.17
  151.2 8.0 %collective-permute-start.3 = (bf16[128,1024]{1,0:T(8,128)(2,1)}, bf16[128,1024]{1,0:T(8,128)(2,1)}, u32[]{:S(2)}, u32[]{:S(2)}) collective-permute-start(bf16[128,1024]{1,0:T(8,128)(2,1)} %collective-permute-done.2), channel_id=1, source_target_pairs={{0,64},{64,128},{128,192},{192,256},{256,320},{320,384},{384,448},... | collective-permute-start | bytes 786440 | tf_op jit(solution)/shard_map/ppermute | solution.py:18
  162.6 7.2 %collective-permute-start.4 = (bf16[128,1024]{1,0:T(8,128)(2,1)}, bf16[128,1024]{1,0:T(8,128)(2,1)S(1)}, u32[]{:S(2)}, u32[]{:S(2)}) collective-permute-start(bf16[128,1024]{1,0:T(8,128)(2,1)} %collective-permute-done.3), channel_id=1, source_target_pairs={{0,64},{64,128},{128,192},{192,256},{256,320},{320,384},{384,448},... | collective-permute-start | bytes 786440 | tf_op jit(solution)/shard_map/ppermute | solution.py:18
  172.8 7.9 %collective-permute-start.5 = (bf16[128,1024]{1,0:T(8,128)(2,1)}, bf16[128,1024]{1,0:T(8,128)(2,1)S(1)}, u32[]{:S(2)}, u32[]{:S(2)}) collective-permute-start(bf16[128,1024]{1,0:T(8,128)(2,1)} %copy-done.28), channel_id=1, source_target_pairs={{0,64},{64,128},{128,192},{192,256},{256,320},{320,384},{384,448},... | collective-permute-start | bytes 786440 | tf_op jit(solution)/shard_map/ppermute | solution.py:18
  183.8 8.1 %collective-permute-start.6 = (bf16[128,1024]{1,0:T(8,128)(2,1)}, bf16[128,1024]{1,0:T(8,128)(2,1)S(1)}, u32[]{:S(2)}, u32[]{:S(2)}) collective-permute-start(bf16[128,1024]{1,0:T(8,128)(2,1)} %copy-done.27), channel_id=1, source_target_pairs={{0,64},{64,128},{128,192},{192,256},{256,320},{320,384},{384,448},... | collective-permute-start | bytes 786440 | tf_op jit(solution)/shard_map/ppermute | solution.py:18
  194.3 3.1 copy-start.2
  194.3 3.1 copy-start.9
  194.3 3.1 copy-start.30
  206.0 9.1 %collective-permute-start.7 = (bf16[128,1024]{1,0:T(8,128)(2,1)}, bf16[128,1024]{1,0:T(8,128)(2,1)}, u32[]{:S(2)}, u32[]{:S(2)}) collective-permute-start(bf16[128,1024]{1,0:T(8,128)(2,1)} %pad_maximum_fusion), channel_id=1, source_target_pairs={{64,0},{128,64},{192,128},{256,192},{320,256},{384,320},{448,384},... | collective-permute-start | bytes 786440 | tf_op jit(solution)/shard_map/ppermute | solution.py:18
  216.9 9.1 %collective-permute-start.8 = (bf16[128,1024]{1,0:T(8,128)(2,1)}, bf16[128,1024]{1,0:T(8,128)(2,1)}, u32[]{:S(2)}, u32[]{:S(2)}) collective-permute-start(bf16[128,1024]{1,0:T(8,128)(2,1)} %fusion.48), channel_id=1, source_target_pairs={{64,0},{128,64},{192,128},{256,192},{320,256},{384,320},{448,384},... | collective-permute-start | bytes 786440 | tf_op jit(solution)/shard_map/ppermute | solution.py:18
  227.9 9.2 %collective-permute-start.9 = (bf16[128,1024]{1,0:T(8,128)(2,1)}, bf16[128,1024]{1,0:T(8,128)(2,1)}, u32[]{:S(2)}, u32[]{:S(2)}) collective-permute-start(bf16[128,1024]{1,0:T(8,128)(2,1)} %fusion.49), channel_id=1, source_target_pairs={{64,0},{128,64},{192,128},{256,192},{320,256},{384,320},{448,384},... | collective-permute-start | bytes 786440 | tf_op jit(solution)/shard_map/ppermute | solution.py:18
  231.6 11.1 %copy-start.3 = (bf16[1,128,512]{1,2,0:T(8,128)(2,1)S(1)}, bf16[1,128,512]{1,2,0:T(8,128)(2,1)}, u32[]{:S(2)}) copy-start(bf16[1,128,512]{1,2,0:T(8,128)(2,1)} %copy.412) | copy-start | bytes 393220
  238.9 8.3 %collective-permute-start.10 = (bf16[128,1024]{1,0:T(8,128)(2,1)}, bf16[128,1024]{1,0:T(8,128)(2,1)}, u32[]{:S(2)}, u32[]{:S(2)}) collective-permute-start(bf16[128,1024]{1,0:T(8,128)(2,1)} %fusion.50), channel_id=1, source_target_pairs={{64,0},{128,64},{192,128},{256,192},{320,256},{384,320},{448,384},... | collective-permute-start | bytes 786440 | tf_op jit(solution)/shard_map/ppermute | solution.py:18
  249.1 8.0 %collective-permute-start.11 = (bf16[128,1024]{1,0:T(8,128)(2,1)}, bf16[128,1024]{1,0:T(8,128)(2,1)}, u32[]{:S(2)}, u32[]{:S(2)}) collective-permute-start(bf16[128,1024]{1,0:T(8,128)(2,1)} %fusion.51), channel_id=1, source_target_pairs={{64,0},{128,64},{192,128},{256,192},{320,256},{384,320},{448,384},... | collective-permute-start | bytes 786440 | tf_op jit(solution)/shard_map/ppermute | solution.py:18
  258.9 8.0 %collective-permute-start.12 = (bf16[128,1024]{1,0:T(8,128)(2,1)}, bf16[128,1024]{1,0:T(8,128)(2,1)}, u32[]{:S(2)}, u32[]{:S(2)}) collective-permute-start(bf16[128,1024]{1,0:T(8,128)(2,1)} %fusion.52), channel_id=1, source_target_pairs={{64,0},{128,64},{192,128},{256,192},{320,256},{384,320},{448,384},... | collective-permute-start | bytes 786440 | tf_op jit(solution)/shard_map/ppermute | solution.py:18
  266.3 13.4 %copy-start.39 = (f32[1024]{0:T(1024)S(1)}, f32[1024]{0:T(1024)}, u32[]{:S(2)}) copy-start(f32[1024]{0:T(1024)} %param.17) | copy-start | bytes 12292
  268.8 9.8 %collective-permute-start.13 = (bf16[128,1024]{1,0:T(8,128)(2,1)}, bf16[128,1024]{1,0:T(8,128)(2,1)}, u32[]{:S(2)}, u32[]{:S(2)}) collective-permute-start(bf16[128,1024]{1,0:T(8,128)(2,1)} %fusion.53), channel_id=1, source_target_pairs={{64,0},{128,64},{192,128},{256,192},{320,256},{384,320},{448,384},... | collective-permute-start | bytes 786440 | tf_op jit(solution)/shard_map/ppermute | solution.py:18
  279.7 2.7 copy-start.5
  284.7 29.9 %copy-start.10 = (bf16[16,4,8,128]{3,2,1,0:T(8,128)(2,1)S(1)}, bf16[16,4,8,128]{3,2,1,0:T(8,128)(2,1)}, u32[]{:S(2)}) copy-start(bf16[16,4,8,128]{3,2,1,0:T(8,128)(2,1)} %get-tuple-element.36) | copy-start | bytes 393220
  305.3 34.6 %all-to-all-start.2 = ((bf16[64,4,1024]{2,1,0:T(4,128)(2,1)}), bf16[64,4,1024]{2,1,0:T(4,128)(2,1)}, u32[]{:S(2)}, u32[]{:S(2)}) async-start(bf16[64,4,1024]{2,1,0:T(4,128)(2,1)} %convert_element_type.226), calls=%async_computation.2 | async-start | bytes 1048576 | tf_op jit(solution)/shard_map/all_to_all | solution.py:209
  311.1 103.9 %all-reduce.2.cloned.1.call-start = ((), (), s32[]{:S(2)}) async-start(), calls=%async_computation.3 | async-start | bytes 262144 | tf_op jit(solution)/shard_map/psum | solution.py:222
  314.6 6.2 %copy-start.11 = (bf16[16,4,8,128]{3,2,1,0:T(8,128)(2,1)S(1)}, bf16[16,4,8,128]{3,2,1,0:T(8,128)(2,1)}, u32[]{:S(2)}) copy-start(bf16[16,4,8,128]{3,2,1,0:T(8,128)(2,1)} %get-tuple-element.43) | copy-start | bytes 393220
  314.6 6.2 %copy-start.14 = (bf16[4,128,128]{2,1,0:T(8,128)(2,1)S(1)}, bf16[4,128,128]{2,1,0:T(8,128)(2,1)}, u32[]{:S(2)}) copy-start(bf16[4,128,128]{2,1,0:T(8,128)(2,1)} %get-tuple-element.66) | copy-start | bytes 393220
  314.6 6.4 %copy-start.12 = (bf16[16,4,8,128]{3,2,1,0:T(8,128)(2,1)S(1)}, bf16[16,4,8,128]{3,2,1,0:T(8,128)(2,1)}, u32[]{:S(2)}) copy-start(bf16[16,4,8,128]{3,2,1,0:T(8,128)(2,1)} %get-tuple-element.41) | copy-start | bytes 393220
  314.6 6.4 %copy-start.13 = (bf16[4,128,128]{2,1,0:T(8,128)(2,1)S(1)}, bf16[4,128,128]{2,1,0:T(8,128)(2,1)}, u32[]{:S(2)}) copy-start(bf16[4,128,128]{2,1,0:T(8,128)(2,1)} %get-tuple-element.67) | copy-start | bytes 393220
  315.8 28.0 %copy-start.7 = (bf16[4,128,128]{2,1,0:T(8,128)(2,1)S(1)}, bf16[4,128,128]{2,1,0:T(8,128)(2,1)}, u32[]{:S(2)}) copy-start(bf16[4,128,128]{2,1,0:T(8,128)(2,1)} %get-tuple-element.61) | copy-start | bytes 393220
  318.3 97.7 %copy-start.38 = (f32[64]{0:T(128)S(1)}, f32[64]{0:T(128)}, u32[]{:S(2)}) copy-start(f32[64]{0:T(128)} %param.15) | copy-start | bytes 772
  (11 other events, 9.4 us)
Sparse Core Ops, SparseCore 0:
  344.0 70.9 all-reduce.1
where the time goes:
time: 428 us; the launch traced here: 424 us
  waiting for transfers between devices  109 us (25%)
  local copies, waits for them, and re-layouts  104 us (24%)
  matrix products  79.6 us (19%)
  starting transfers between devices  53.3 us (12%)
  blocking collectives  32.5 us (8%)
  other arithmetic  30.7 us (7%)
  between operations  14.9 us (3%)
    psum x1, waiting for transfers between devices, per_device(): lax.psum(local_grad.astype(jnp.bfloat16), 'ctx').astype(jnp.float32)  67.5 us
    ppermute x14, starting transfers between devices, passed_along(): return lax.ppermute(value, axis, pairs)  42.1 us
    all_to_all x1, blocking collectives, per_device(): lax.all_to_all(requests, 'tab', split_axis=0, concat_axis=0, tiled=True)  32.5 us
    all_to_all x1, waiting for transfers between devices, per_device(): lax.all_to_all(served, 'tab', split_axis=0, concat_axis=0, tiled=True)  21.1 us
    scatter x1, local copies, waits for them, and re-layouts, per_device(): outgoing = jnp.zeros((tab_peers, capacity, model_width), jnp.float32).at[...  18.4 us
    all_to_all x1, waiting for transfers between devices, per_device(): lax.all_to_all(outgoing.astype(jnp.bfloat16), 'tab', split_axis=0, concat...  17.9 us
    unnamed x93, local copies, waits for them, and re-layouts  17.4 us
    dot_general x8, matrix products, backward_tile(): jnp.einsum('hqk,khd->qhd', grad_raw, key_part, preferred_element_type=jnp...  15.6 us
  transfers between devices with their start and end apart: 17, of which 6 were waited for; matrix products, arithmetic and copies ran while one was open for 23% of the time, Pallas kernels for 0%

commit v1 on v0

v1 whole, which is shorter than its diff:
```python
import functools
import math

import jax
import jax.numpy as jnp
from jax import lax
from jax.experimental import pallas as pl
from jax.experimental.pallas import tpu as pltpu
from jax.sharding import PartitionSpec as P

MESH = pl.DeviceIdType.MESH
F32 = jnp.float32
BF16 = jnp.bfloat16
I32 = jnp.int32

NORM_EPS = 1e-05
LEARN_RATE = 0.1

CTX = 8
Y = 4
B = 128
ROWS = 64
PLANE = Y * ROWS
MODEL = 1024
HEADS = 4
CHUNKS = 2
PIECE = PLANE // CHUNKS
SPLIT = 3
REACH = 5
SCALE = 1.0 / math.sqrt(B)
FAR_FIRST = (4, 3, 5, 2, 6, 1, 7)

NT = (((1,), (1,)), ((), ()))
TN = (((0,), (0,)), ((), ()))


def dot(a, b, dims=(((1,), (0,)), ((), ()))):
    return lax.dot_general(a, b, dims, preferred_element_type=F32)


def kernel(
    planes,
    item_ref, act_ref, hist_ref, masters_ref, accum_ref, atab_ref, gain_ref, w_ref, dout_ref,
    att_out, rg_out, nm_out, na_out,
    mslice, mfull, w_v, tbl, ids, itemb, gacc, g1, x1, xin, hn, startb, invb,
    pd, stq, stkv, qb, kvb, dob, attacc, dqacc, dqs, dkvs, atts, rdq, rdkv, ratt, dqf, gh,
    g2, gin, sb, rb, own, yb, fin,
    loc_s, y_s, y_r, z_s, z_r, id_s, id_r, a1_s, a1_r, q_s, q_r, kv_s, kv_r, do_s, do_r,
    dq_s, dq_r, dkv_s, dkv_r, at_s, at_r, a2_s, a2_r, rs_s, rs_r, ry_s, ry_r, f_s, f_r,
):
    half = planes // 2
    c = lax.axis_index("ctx")
    t = lax.axis_index("tab")
    x, core = lax.div(c, 2), lax.rem(c, 2)
    z, y = lax.div(t, Y), lax.rem(t, Y)

    def ctx_at(d):
        return lax.rem(c + d, CTX)

    def tab_y(d):
        return z * Y + lax.rem(y + d + Y, Y)

    def z_at(d):
        return lax.rem(z + d + 2 * planes, planes)

    def tab_z(d):
        return z_at(d) * Y + y

    def remote(src, dst, ssem, rsem, to_ctx, to_tab):
        return pltpu.make_async_remote_copy(
            src_ref=src, dst_ref=dst, send_sem=ssem, recv_sem=rsem,
            device_id=(to_ctx, to_tab), device_id_type=MESH,
        )

    def got(dst, rsem, ssem):
        remote(dst, dst, ssem, rsem, c, t).wait_recv()

    def sent(src, ssem, rsem):
        remote(src, src, ssem, rsem, c, t).wait_send()

    cp_slice = pltpu.make_async_copy(
        masters_ref.at[:, pl.ds(pl.multiple_of(c * B, B), B)], mslice, loc_s.at[0]
    )
    cp_slice.start()
    cp_full = pltpu.make_async_copy(masters_ref, mfull, loc_s.at[1])
    cp_w = []
    for h in range(HEADS):
        for part in range(3):
            cp_w.append(
                pltpu.make_async_copy(
                    w_ref.at[:, pl.ds(part * HEADS * B + h * B, B)],
                    w_v.at[h, :, pl.ds(part * B, B)],
                    loc_s.at[2 + 3 * h + part],
                )
            )

    barrier = pltpu.get_barrier_semaphore()
    for d in (1, -1):
        pl.semaphore_signal(barrier, inc=1, device_id=(c, tab_z(d)), device_id_type=MESH)
    for d in range(1, Y):
        pl.semaphore_signal(barrier, inc=1, device_id=(c, tab_y(d)), device_id_type=MESH)
    for d in range(1, CTX):
        pl.semaphore_signal(barrier, inc=1, device_id=(ctx_at(d), t), device_id_type=MESH)

    item = item_ref[...]
    owner, row = lax.shift_right_logical(item, 6), item & 63
    place = (
        lax.shift_right_logical(owner, 2) * PLANE + ((y + Y - (owner & 3)) & 3) * ROWS + row
    )
    ids[c] = jnp.broadcast_to(place, (8, B))

    cp_slice.wait()
    tbl[z, 0:ROWS, :] = mslice[...].astype(BF16)
    pl.semaphore_wait(barrier, CTX - 1 + Y - 1 + 2)

    for d in (2, 1, 3):
        remote(
            tbl.at[z, pl.ds(0, ROWS)], tbl.at[z, pl.ds(d * ROWS, ROWS)],
            y_s.at[d - 1], y_r.at[d - 1], c, tab_y(d),
        ).start()
    for d in FAR_FIRST:
        remote(ids.at[c], ids.at[c], id_s.at[d - 1], id_r.at[d - 1], ctx_at(d), t).start()

    def ring_send(side, k, n):
        plane = z_at(-k) if side == 0 else z_at(k)
        block = tbl.at[plane, pl.ds(n * PIECE, PIECE)]
        return remote(
            block, block, z_s.at[side, k, n], z_r.at[side, k, n], c, tab_z(1 if side == 0 else -1)
        )

    def ring_got(side, k, n):
        plane = z_at(-1 - k) if side == 0 else z_at(1 + k)
        got(tbl.at[plane, pl.ds(n * PIECE, PIECE)], z_r.at[side, k, n], z_s.at[side, k, n])

    def far_side(n):
        return 0 if n < CHUNKS // 2 else 1

    per_piece = Y // CHUNKS
    for n in range(CHUNKS):
        for d in range(n * per_piece, (n + 1) * per_piece):
            if d:
                got(tbl.at[z, pl.ds(d * ROWS, ROWS)], y_r.at[d - 1], y_s.at[d - 1])
        for side in range(2):
            ring_send(side, 0, n).start()

    def to_heads(src_of, dst, ssem, rsem, local):
        for r in (2, 1, 3, 0):
            h = lax.rem(x + r, HEADS)
            for s in range(2):
                need = (c <= SPLIT + REACH - 2) if s == 0 else (c >= SPLIT)
                dev = 2 * h + s

                @pl.when(need & (dev != c))
                def _():
                    remote(src_of(h), dst.at[c], ssem.at[h, s], rsem.at[c], dev, t).start()

                @pl.when(need & (dev == c))
                def _():
                    local(h)

    def dout_of(h):
        return dout_ref.at[:, pl.ds(pl.multiple_of(h * B, B), B)]

    def dout_here(h):
        dob[c] = dout_ref[:, pl.ds(pl.multiple_of(h * B, B), B)]

    to_heads(dout_of, dob, do_s, do_r, dout_here)
    for copy in cp_w:
        copy.start()
    cp_full.start()

    actb = jnp.broadcast_to(act_ref[...], (B, B)).T
    for j in range(8):
        block = pl.ds(j * B, B)
        emb = jnp.broadcast_to(atab_ref[0:1, block], (B, B))
        for a in range(1, 8):
            emb = jnp.where(actb == a, atab_ref[a : a + 1, block], emb)
        xin[j] = emb
    h0, h1, h2, h3 = hist_ref[0, 0], hist_ref[0, 1], hist_ref[0, 2], hist_ref[0, 3]
    e0, e1, e2 = h0, h0 + h1, h0 + h1 + h2

    def spans(i, carry):
        p = lax.broadcasted_iota(I32, (B, B), 0) + i * B
        in0, in1, in2 = p < e0, p < e1, p < e2
        startb[i] = jnp.where(in0, 0, jnp.where(in1, e0, jnp.where(in2, e1, e2)))
        length = jnp.where(in0, h0, jnp.where(in1, h1, jnp.where(in2, h2, h3)))
        invb[i] = 1.0 / length.astype(F32)
        return carry

    lax.fori_loop(0, 8, spans, 0)
    for d in range(1, CTX):
        src = ctx_at(CTX - d)
        got(ids.at[src], id_r.at[d - 1], id_s.at[d - 1])

    def spread(j, carry):
        itemb[j] = jnp.broadcast_to(ids[j, 0:1, :], (B, B)).T
        gacc[j] = jnp.zeros((B, B), F32)
        return carry

    lax.fori_loop(0, 8, spread, 0)

    lane = lax.broadcasted_iota(I32, (2 * B, B), 1)

    def gather_plane(plane):
        rows = tbl[plane]
        base = plane * PLANE

        def some(i, carry):
            at = pl.ds(2 * i, 2)
            wanted = itemb[at].reshape(2 * B, B) - base
            hot = jnp.concatenate(
                [jnp.where(wanted == lane + k * B, 1.0, 0.0).astype(BF16) for k in range(2)], axis=1
            )
            gacc[at] = gacc[at] + dot(hot, rows).reshape(2, B, B)
            return carry

        lax.fori_loop(0, 4, some, 0)

    gather_plane(z)

    def ring_step(k, last):
        for n in range(CHUNKS):
            for side in range(2):
                ring_got(side, k - 1, n)
                if not last or far_side(n) == side:
                    ring_send(side, k, n).start()
        gather_plane(z_at(-k))
        gather_plane(z_at(k))

    def ring_body(k, carry):
        ring_step(k, False)
        return carry

    lax.fori_loop(1, half - 1, ring_body, 0)
    ring_step(half - 1, True)
    for n in range(CHUNKS):
        ring_got(far_side(n), half - 1, n)
    gather_plane(z_at(half))

    for j in range(8):
        g1[j] = gacc[j].astype(BF16)
    for d in FAR_FIRST:
        dst = ctx_at(d)
        remote(g1.at[dst], x1.at[c], a1_s.at[d - 1], a1_r.at[d - 1], dst, t).start()
    x1[c] = g1[c]
    for d in range(1, CTX):
        src = ctx_at(CTX - d)
        got(x1.at[src], a1_r.at[d - 1], a1_s.at[d - 1])

    total = jnp.zeros((B, B), F32)
    for j in range(8):
        value = xin[j] + x1[j].astype(F32)
        xin[j] = value
        total = total + value
    mean = jnp.sum(total, axis=1, keepdims=True) * (1.0 / MODEL)
    total = jnp.zeros((B, B), F32)
    for j in range(8):
        centre = xin[j] - mean
        total = total + centre * centre
    inv_std = lax.rsqrt(jnp.sum(total, axis=1, keepdims=True) * (1.0 / MODEL) + NORM_EPS)
    for j in range(8):
        normed = (xin[j] - mean) * inv_std
        xin[j] = normed
        hn[:, j * B : (j + 1) * B] = (normed * gain_ref[:, j * B : (j + 1) * B]).astype(BF16)
    for copy in cp_w:
        copy.wait()

    def q_of(h):
        return stq.at[h]

    def q_here(h):
        qb[c] = stq[h]

    holder = jnp.where(c >= SPLIT, 1, 0)
    for r in (2, 1, 3, 0):
        h = lax.rem(x + r, HEADS)
        project = dot(hn[...], w_v[h])
        sig = jax.nn.sigmoid(project)
        pd[h] = sig * (1.0 + project * (1.0 - sig))
        active = (project * sig).astype(BF16)
        stq[h] = active[:, 0:B]
        stkv[h] = active[:, B : 3 * B]
        dev = 2 * h + holder

        @pl.when(dev != c)
        def _():
            remote(stkv.at[h], kvb.at[c], kv_s.at[h], kv_r.at[c], dev, t).start()

        @pl.when(dev == c)
        def _():
            kvb[c] = stkv[h]

        for s in (1, 0):
            need = (c <= SPLIT + REACH - 2) if s == 0 else (c >= SPLIT)
            to = 2 * h + s

            @pl.when(need & (to != c))
            def _():
                remote(stq.at[h], qb.at[c], q_s.at[h, s], q_r.at[c], to, t).start()

            @pl.when(need & (to == c))
            def _():
                q_here(h)

    def send_back(stage, ssem, rsem, dst, block):
        @pl.when(c != block)
        def _():
            remote(stage.at[block], dst, ssem.at[block], rsem, block, t).start()

        @pl.when(c == block)
        def _():
            dst[...] = stage[block]

    def attend(s):
        key_blocks = range(0, SPLIT) if s == 0 else range(SPLIT, 8)
        lowest = key_blocks[0]
        query_blocks = range(0, SPLIT + REACH - 1) if s == 0 else range(SPLIT, 8)
        waited = set()
        for kb in key_blocks:
            end = min(kb + REACH, 8)
            n = (end - kb) * B

            @pl.when(c != kb)
            def _():
                got(kvb.at[kb], kv_r.at[kb], kv_s.at[0])

            for b in range(kb, end):
                if b not in waited:
                    waited.add(b)

                    @pl.when(c != b)
                    def _():
                        got(qb.at[b], q_r.at[b], q_s.at[0, 0])
                        got(dob.at[b], do_r.at[b], do_s.at[0, 0])

            queries = qb[kb:end].reshape(n, B)
            grad_out = dob[kb:end].reshape(n, B)
            keys = kvb[kb, :, 0:B]
            values = kvb[kb, :, B : 2 * B]
            raw = dot(queries, keys, NT) * SCALE
            sig = jax.nn.sigmoid(raw)
            inv = invb[kb:end].reshape(n, B)
            k_pos = lax.broadcasted_iota(I32, (n, B), 1) + kb * B
            q_pos = lax.broadcasted_iota(I32, (n, B), 0) + kb * B
            allowed = (k_pos >= startb[kb:end].reshape(n, B)) & (k_pos <= q_pos)
            weights = jnp.where(allowed, raw * sig * inv, 0.0).astype(BF16)
            grad_w = dot(grad_out, values, NT)
            slope = sig * (1.0 + raw * (1.0 - sig))
            grad_raw = jnp.where(allowed, grad_w * slope * (inv * SCALE), 0.0).astype(BF16)
            dkvs[kb, :, 0:B] = dot(grad_raw, queries, TN).astype(BF16)
            dkvs[kb, :, B : 2 * B] = dot(weights, grad_out, TN).astype(BF16)
            send_back(dkvs, dkv_s, dkv_r.at[x], rdkv.at[x], kb)
            dq = dot(grad_raw, keys)
            at = dot(weights, values)
            for b in range(kb, end):
                rows = slice((b - kb) * B, (b - kb + 1) * B)
                first = kb == max(b - REACH + 1, lowest)
                last = kb == min(b, key_blocks[-1])
                dq_b = dq[rows] if first else dqacc[b] + dq[rows]
                at_b = at[rows] if first else attacc[b] + at[rows]
                if last:
                    dqs[b] = dq_b.astype(BF16)
                    send_back(dqs, dq_s, dq_r.at[s, x], rdq.at[s, x], b)
                    atts[b] = at_b.astype(BF16)
                else:
                    dqacc[b] = dq_b
                    attacc[b] = at_b
        for b in query_blocks:
            send_back(atts, at_s, at_r.at[s, x], ratt.at[s, x], b)

    for s in range(2):
        @pl.when(core == s)
        def _():
            attend(s)

    both = (c >= SPLIT) & (c <= SPLIT + REACH - 2)
    for r in (0, 1, 3, 2):
        h = lax.rem(x + r, HEADS)

        @pl.when(2 * h + holder != c)
        def _():
            got(rdkv.at[h], dkv_r.at[h], dkv_s.at[0])
            got(rdq.at[holder, h], dq_r.at[holder, h], dq_s.at[0])

        @pl.when(both & (2 * h != c))
        def _():
            got(rdq.at[0, h], dq_r.at[0, h], dq_s.at[0])

        dqf[...] = rdq[holder, h].astype(F32)

        @pl.when(both)
        def _():
            dqf[...] = dqf[...] + rdq[0, h].astype(F32)

        slope = pd[h]
        grad_project = jnp.concatenate(
            [
                (dqf[...] * slope[:, 0:B]).astype(BF16),
                (rdkv[h].astype(F32) * slope[:, B : 3 * B]).astype(BF16),
            ],
            axis=1,
        )
        part = dot(grad_project, w_v[h], NT)
        gh[...] = part if r == 0 else gh[...] + part

    total = jnp.zeros((B, B), F32)
    cross = jnp.zeros((B, B), F32)
    for j in range(8):
        cols = slice(j * B, (j + 1) * B)
        g = gh[:, cols] * gain_ref[:, cols]
        gh[:, cols] = g
        total = total + g
        cross = cross + g * xin[j]
    mean_g = jnp.sum(total, axis=1, keepdims=True) * (1.0 / MODEL)
    mean_c = jnp.sum(cross, axis=1, keepdims=True) * (1.0 / MODEL)
    for j in range(8):
        g = gh[:, j * B : (j + 1) * B]
        g2[j] = (inv_std * (g - mean_g - xin[j] * mean_c)).astype(BF16)

    for d in FAR_FIRST:
        dst = ctx_at(d)
        remote(g2.at[dst], gin.at[c], a2_s.at[d - 1], a2_r.at[d - 1], dst, t).start()
    gin[c] = g2[c]
    for d in range(1, CTX):
        src = ctx_at(CTX - d)
        got(gin.at[src], a2_r.at[d - 1], a2_s.at[d - 1])

    sub = lax.broadcasted_iota(I32, (PLANE, B), 0)

    def plane_sum(plane):
        base = plane * PLANE
        hot = jnp.concatenate(
            [jnp.where(ids[j, 0:1, :] - base == sub, 1.0, 0.0).astype(BF16) for j in range(8)],
            axis=1,
        )
        return dot(hot, gin[...].reshape(8 * B, B))

    def reduce_send(side, k, n):
        at = pl.ds(n * PIECE, PIECE)
        return remote(
            sb.at[side, k, at], rb.at[side, k, at], rs_s.at[side, k, n], rs_r.at[side, k, n],
            c, tab_z(1 if side == 0 else -1),
        )

    def reduce_got(side, k, n):
        got(rb.at[side, k, pl.ds(n * PIECE, PIECE)], rs_r.at[side, k, n], rs_s.at[side, k, n])

    first_sum = plane_sum(z_at(half))
    for n in range(CHUNKS):
        rows = slice(n * PIECE, (n + 1) * PIECE)
        sb[far_side(n), 0, rows, :] = first_sum[rows].astype(BF16)
        reduce_send(far_side(n), 0, n).start()

    def reduce_step(k, first):
        for side in range(2):
            own[side] = plane_sum(z_at(half - k) if side == 0 else z_at(k - half))
        for n in range(CHUNKS):
            rows = slice(n * PIECE, (n + 1) * PIECE)
            for side in range(2):
                value = own[side, rows, :]
                if not first or far_side(n) == side:
                    reduce_got(side, k - 1, n)
                    value = value + rb[side, k - 1, rows, :].astype(F32)
                sb[side, k, rows, :] = value.astype(BF16)
                reduce_send(side, k, n).start()

    def reduce_body(k, carry):
        reduce_step(k, False)
        return carry

    reduce_step(1, True)
    lax.fori_loop(2, half, reduce_body, 0)
    own[0] = plane_sum(z)

    for h in range(HEADS):
        @pl.when(2 * h + holder != c)
        def _():
            got(ratt.at[holder, h], at_r.at[holder, h], at_s.at[0])

        @pl.when(both & (2 * h != c))
        def _():
            got(ratt.at[0, h], at_r.at[0, h], at_s.at[0])

        dqf[...] = ratt[holder, h].astype(F32)

        @pl.when(both)
        def _():
            dqf[...] = dqf[...] + ratt[0, h].astype(F32)

        att_out[:, h * B : (h + 1) * B] = dqf[...].astype(BF16)

    for n in range(CHUNKS):
        rows = slice(n * PIECE, (n + 1) * PIECE)
        value = own[0, rows, :]
        for side in range(2):
            reduce_got(side, half - 1, n)
            value = value + rb[side, half - 1, rows, :].astype(F32)
        own[0, rows, :] = value

    for d in (2, 1, 3):
        yb[0, d - 1] = own[0, d * ROWS : (d + 1) * ROWS, :].astype(BF16)
        remote(
            yb.at[0, d - 1], yb.at[1, d - 1], ry_s.at[d - 1], ry_r.at[d - 1], c, tab_y(-d)
        ).start()
    value = own[0, 0:ROWS, :]
    for d in (1, 3, 2):
        got(yb.at[1, d - 1], ry_r.at[d - 1], ry_s.at[d - 1])
        value = value + yb[1, d - 1].astype(F32)

    fin[c] = value.astype(BF16)
    for d in FAR_FIRST:
        remote(fin.at[c], fin.at[c], f_s.at[d - 1], f_r.at[d - 1], ctx_at(d), t).start()
    cp_full.wait()
    for d in range(1, CTX):
        src = ctx_at(CTX - d)
        got(fin.at[src], f_r.at[d - 1], f_s.at[d - 1])

    total = jnp.zeros((ROWS, B), F32)
    for j in range(8):
        g = fin[j].astype(F32)
        rg_out[:, j * B : (j + 1) * B] = g
        total = total + g * g
    diagonal = lax.broadcasted_iota(I32, (ROWS, ROWS), 0) == lax.broadcasted_iota(
        I32, (ROWS, ROWS), 1
    )
    before = jnp.sum(jnp.where(diagonal, accum_ref[...], 0.0), axis=1, keepdims=True)
    after = before + jnp.sum(total, axis=1, keepdims=True) * (1.0 / MODEL)
    na_out[...] = jnp.sum(jnp.where(diagonal, after, 0.0), axis=0, keepdims=True)
    rate = LEARN_RATE * lax.rsqrt(after)
    for j in range(8):
        cols = slice(j * B, (j + 1) * B)
        nm_out[:, cols] = mfull[:, cols] - fin[j].astype(F32) * rate

    for d in range(1, Y):
        sent(tbl.at[z, pl.ds(0, ROWS)], y_s.at[d - 1], y_r.at[d - 1])
        sent(yb.at[0, d - 1], ry_s.at[d - 1], ry_r.at[d - 1])
    for d in range(1, CTX):
        sent(ids.at[c], id_s.at[d - 1], id_r.at[d - 1])
        sent(g1.at[0], a1_s.at[d - 1], a1_r.at[d - 1])
        sent(g2.at[0], a2_s.at[d - 1], a2_r.at[d - 1])
        sent(fin.at[c], f_s.at[d - 1], f_r.at[d - 1])
    for side in range(2):
        for n in range(CHUNKS):
            for k in range(half):
                if k < half - 1 or far_side(n) == side:
                    ring_send(side, k, n).wait_send()
                if k > 0 or far_side(n) == side:
                    reduce_send(side, k, n).wait_send()
    for h in range(HEADS):
        @pl.when(2 * h + holder != c)
        def _():
            sent(stkv.at[h], kv_s.at[h], kv_r.at[0])

        for s in range(2):
            need = (c <= SPLIT + REACH - 2) if s == 0 else (c >= SPLIT)

            @pl.when(need & (2 * h + s != c))
            def _():
                sent(stq.at[h], q_s.at[h, s], q_r.at[0])
                sent(dob.at[0], do_s.at[h, s], do_r.at[0])

    for b in range(8):
        @pl.when((c != b) & (core == (0 if b < SPLIT else 1)))
        def _():
            sent(dkvs.at[b], dkv_s.at[b], dkv_r.at[0])

        for s in range(2):
            need = b <= SPLIT + REACH - 2 if s == 0 else b >= SPLIT
            if need:
                @pl.when((c != b) & (core == s))
                def _():
                    sent(dqs.at[b], dq_s.at[b], dq_r.at[0, 0])
                    sent(atts.at[b], at_s.at[b], at_r.at[0, 0])


def per_device(
    item_owner, item_row, action_id, history_len, masters, row_accum, action_table, norm_gain,
    w_qkv, d_attended,
):
    planes = lax.axis_size("tab") // Y
    half = planes // 2
    item = item_owner[0, :, 0][None, :] * ROWS + item_row
    vmem = pl.BlockSpec(memory_space=pltpu.VMEM)
    smem = pl.BlockSpec(memory_space=pltpu.SMEM)
    hbm = pl.BlockSpec(memory_space=pl.ANY)
    dma = pltpu.SemaphoreType.DMA

    def block(*lead, rows=B, cols=B, dtype=BF16):
        return pltpu.VMEM((*lead, rows, cols), dtype)

    scratch = [
        pltpu.VMEM((ROWS, B), F32),
        pltpu.VMEM((ROWS, MODEL), F32),
        pltpu.VMEM((HEADS, MODEL, 3 * B), BF16),
        block(planes, rows=PLANE),
        block(8, rows=8, dtype=I32),
        block(8, dtype=I32),
        block(8, dtype=F32),
        block(8),
        block(8),
        block(8, dtype=F32),
        block(cols=MODEL),
        block(8, dtype=I32),
        block(8, dtype=F32),
        block(HEADS, cols=3 * B, dtype=F32),
        block(HEADS),
        block(HEADS, cols=2 * B),
        block(8),
        block(8, cols=2 * B),
        block(8),
        block(8, dtype=F32),
        block(8, dtype=F32),
        block(8),
        block(8, cols=2 * B),
        block(8),
        block(2, HEADS),
        block(HEADS, cols=2 * B),
        block(2, HEADS),
        block(dtype=F32),
        block(cols=MODEL, dtype=F32),
        block(8),
        block(8),
        block(2, half, rows=PLANE),
        block(2, half, rows=PLANE),
        block(2, rows=PLANE, dtype=F32),
        block(2, Y - 1, rows=ROWS),
        block(8, rows=ROWS),
        dma((14,)),
        dma((Y - 1,)), dma((Y - 1,)),
        dma((2, half, CHUNKS)), dma((2, half, CHUNKS)),
        dma((7,)), dma((7,)),
        dma((7,)), dma((7,)),
        dma((HEADS, 2)), dma((8,)),
        dma((HEADS,)), dma((8,)),
        dma((HEADS, 2)), dma((8,)),
        dma((8,)), dma((2, HEADS)),
        dma((8,)), dma((HEADS,)),
        dma((8,)), dma((2, HEADS)),
        dma((7,)), dma((7,)),
        dma((2, half, CHUNKS)), dma((2, half, CHUNKS)),
        dma((Y - 1,)), dma((Y - 1,)),
        dma((7,)), dma((7,)),
    ]
    attended, row_grads, new_masters, new_accum = pl.pallas_call(
        functools.partial(kernel, planes),
        out_shape=(
            jax.ShapeDtypeStruct((B, HEADS * B), BF16),
            jax.ShapeDtypeStruct((ROWS, MODEL), F32),
            jax.ShapeDtypeStruct((ROWS, MODEL), F32),
            jax.ShapeDtypeStruct((1, ROWS), F32),
        ),
        in_specs=[vmem, vmem, smem, hbm, vmem, vmem, vmem, hbm, vmem],
        out_specs=(vmem, vmem, vmem, vmem),
        scratch_shapes=scratch,
        compiler_params=pltpu.CompilerParams(
            collective_id=0, has_side_effects=True, vmem_limit_bytes=48 * 1024 * 1024
        ),
    )(
        item, action_id, history_len, masters, row_accum[None, :], action_table,
        norm_gain[None, :], w_qkv, d_attended[0],
    )
    return (attended[None], row_grads, new_masters, new_accum[0])


def solution(mesh):
    in_specs = (
        P("tab", "ctx", None),
        P("tab", "ctx"),
        P("tab", "ctx"),
        P("tab", None),
        P("tab", None),
        P("tab"),
        P(),
        P(),
        P(),
        P("tab", "ctx", None),
    )
    out_specs = (P("tab", "ctx", None), P("tab", None), P("tab", None), P("tab"))
    return jax.shard_map(
        per_device, mesh=mesh, in_specs=in_specs, out_specs=out_specs, check_vma=False
    )
```

time: 428 us -> 123 us (0.29)
  Pallas kernels: 0 us -> 112 us
  waiting for transfers between devices: 109 us -> 0 us
  local copies, waits for them, and re-layouts: 104 us -> 9.72 us
  matrix products: 79.6 us -> 0 us
  starting transfers between devices: 53.3 us -> 0 us
  blocking collectives: 32.5 us -> 0 us
  other arithmetic: 30.7 us -> 0.68 us
  between operations: 14.9 us -> 0.65 us
    pallas_call x0 -> x1, Pallas kernels: none -> 112 us  [per_device(): pl.pallas_call(functools.partial(kernel, planes), out_shape=(jax.ShapeDty...]
    dot_general x52 -> x0, matrix products: 79.6 us -> none  [the longest x8 15.6 us: backward_tile(): jnp.einsum('hqk,khd->qhd', grad_raw, key_part, preferred_element_type=jnp...]
    psum x1 -> x0, waiting for transfers between devices: 67.5 us -> none  [per_device(): lax.psum(local_grad.astype(jnp.bfloat16), 'ctx').astype(jnp.float32)]
    reshape x27 -> x0, local copies, waits for them, and re-layouts: 46.5 us -> none  [the longest x8 14.2 us: backward_tile(): grad_key = jnp.einsum('hqk,qhd->khd', grad_raw, queries, preferred_elemen...]
    ppermute x14 -> x0, starting transfers between devices: 42.1 us -> none  [passed_along(): return lax.ppermute(value, axis, pairs)]
    all_to_all x2 -> x0, waiting for transfers between devices: 38.9 us -> none  [the longest x1 21.1 us: per_device(): lax.all_to_all(served, 'tab', split_axis=0, concat_axis=0, tiled=True)]
    all_to_all x1 -> x0, blocking collectives: 32.5 us -> none  [per_device(): lax.all_to_all(requests, 'tab', split_axis=0, concat_axis=0, tiled=True)]
    scatter x2 -> x0, local copies, waits for them, and re-layouts: 29.3 us -> none  [the longest x1 18.4 us: per_device(): outgoing = jnp.zeros((tab_peers, capacity, model_width), jnp.float32).at[...]
  transfers between devices with their start and end apart: 17 -> 0, of which waited for: 6 -> 0; matrix products, arithmetic and copies ran while one was open for 23% -> 0% of each run, Pallas kernels for 0% -> 0%
where the time goes in v1:
time: 123 us
  Pallas kernels  112 us (91%)
  local copies, waits for them, and re-layouts  9.72 us (8%)
    pallas_call x1, Pallas kernels, per_device(): pl.pallas_call(functools.partial(kernel, planes), out_shape=(jax.ShapeDty...  112 us
    unnamed x20, local copies, waits for them, and re-layouts  9.72 us

profile of v1, /device:TPU:1, one launch (start us, length us, event | category | flops | bytes accessed | tf_op | source)
XLA Modules:
  0.0 122.6 jit_solution(5796767366274131857)
XLA Ops:
  0.6 0.7 bitcast_add_fusion.item_ref
  1.3 0.0 copy-start
  1.3 1.9 %copy-done = bf16[1024,1536]{1,0:T(8,128)(2,1)S(1)} copy-done((bf16[1024,1536]{1,0:T(8,128)(2,1)S(1)}, bf16[1024,1536]{1,0:T(8,128)(2,1)}, u32[]{:S(2)}) %copy-start) | copy-done | bytes 3145752
  3.2 0.0 copy-start.1
  3.2 0.9 copy-done.1
  4.1 0.0 copy-start.2
  4.2 0.9 copy-done.2
  5.1 0.0 copy-start.3
  5.1 0.8 copy-done.3
  5.8 0.0 copy-start.4
  5.8 0.7 copy-done.4
  6.5 0.0 copy-start.5
  6.5 0.7 copy-done.5
  7.2 0.0 copy-start.6
  7.2 0.7 copy-done.6
  7.8 0.0 copy-start.7
  7.8 0.7 copy-done.7
  8.5 111.6 %shard_map.129 = (bf16[128,512]{1,0:T(8,128)(2,1)S(1)}, f32[64,1024]{1,0:T(8,128)S(1)}, f32[64,1024]{1,0:T(8,128)S(1)}, f32[1,64]{1,0:T(1,128)S(1)}) custom-call(s32[1,128]{1,0:T(1,128)S(1)} %bitcast_add_fusion.item_ref, s32[1,128]{1,0:T(1,128)S(1)} %copy-done.5, s32[1,4]{1,0:T(1,128)S(1)} %copy-done.6, f32[64,1024]{1,0:T(8,128)S(1)} %copy-done.1, ...), custom_call_target="tpu_custom_call" | custom-call | tf_op jit(solution)/shard_map/pallas_call | solution.py:644
  120.0 0.7 copy.18
  120.7 0.7 copy.19
  121.4 0.7 copy.20
  122.1 0.5 copy.21
Async XLA Ops:
  1.3 1.9 %copy-start = (bf16[1024,1536]{1,0:T(8,128)(2,1)S(1)}, bf16[1024,1536]{1,0:T(8,128)(2,1)}, u32[]{:S(2)}) copy-start(bf16[1024,1536]{1,0:T(8,128)(2,1)} %w_ref.1) | copy-start | bytes 9437188
  3.2 0.9 copy-start.1
  4.1 0.9 copy-start.2
  5.1 0.8 copy-start.3
  5.8 0.7 copy-start.4
  6.5 0.7 copy-start.5
  7.2 0.7 copy-start.6
  7.8 0.7 copy-start.7

commit v2 on v1

--- a/solution.py
+++ b/solution.py
@@ -1,4 +1,3 @@
-import functools
 import math
 
 import jax
@@ -23,8 +22,12 @@
 PLANE = Y * ROWS
 MODEL = 1024
 HEADS = 4
-CHUNKS = 2
-PIECE = PLANE // CHUNKS
+Z = 16
+GROUPS = 4
+SLOTS = (0, 1, -1, 2, -2, 3, -3, 4, -4, 5, -5, 6, -6, 7, -7, 8)
+SLOT_OF = {distance: slot for slot, distance in enumerate(SLOTS)} | {-8: 15}
+LEAP = 4
+HALF = ROWS // 2
 SPLIT = 3
 REACH = 5
 SCALE = 1.0 / math.sqrt(B)
@@ -39,16 +42,16 @@
 
 
 def kernel(
-    planes,
-    item_ref, act_ref, hist_ref, masters_ref, accum_ref, atab_ref, gain_ref, w_ref, dout_ref,
+    owner_hbm, row_hbm, act_hbm, hist_hbm, masters_ref, accum_hbm, atab_hbm, gain_hbm, w_ref,
+    dout_hbm,
     att_out, rg_out, nm_out, na_out,
-    mslice, mfull, w_v, tbl, ids, itemb, gacc, g1, x1, xin, hn, startb, invb,
+    owner_ref, row_ref, act_ref, hist_ref, accum_ref, atab_ref, gain_ref, dout_ref,
+    mslice, mfull, w_v, tbl, ids, high, low, high_row, low_row, gacc, g1, x1, xin, hn, startb, invb,
     pd, stq, stkv, qb, kvb, dob, attacc, dqacc, dqs, dkvs, atts, rdq, rdkv, ratt, dqf, gh,
-    g2, gin, sb, rb, own, yb, fin,
+    g2, gin, psum, own, yb, stage, agg, zb, fin,
     loc_s, y_s, y_r, z_s, z_r, id_s, id_r, a1_s, a1_r, q_s, q_r, kv_s, kv_r, do_s, do_r,
-    dq_s, dq_r, dkv_s, dkv_r, at_s, at_r, a2_s, a2_r, rs_s, rs_r, ry_s, ry_r, f_s, f_r,
+    dq_s, dq_r, dkv_s, dkv_r, at_s, at_r, a2_s, a2_r, ry_s, ry_r, ag_s, ag_r, rz_s, rz_r, f_s, f_r,
 ):
-    half = planes // 2
     c = lax.axis_index("ctx")
     t = lax.axis_index("tab")
     x, core = lax.div(c, 2), lax.rem(c, 2)
@@ -61,7 +64,7 @@
         return z * Y + lax.rem(y + d + Y, Y)
 
     def z_at(d):
-        return lax.rem(z + d + 2 * planes, planes)
+        return lax.rem(z + d + Z, Z)
 
     def tab_z(d):
         return z_at(d) * Y + y
@@ -82,6 +85,21 @@
         masters_ref.at[:, pl.ds(pl.multiple_of(c * B, B), B)], mslice, loc_s.at[0]
     )
     cp_slice.start()
+    cp_ids = []
+    for i, (src, dst) in enumerate(((owner_hbm, owner_ref), (row_hbm, row_ref))):
+        cp_ids.append(pltpu.make_async_copy(src, dst, loc_s.at[14 + i]))
+        cp_ids[-1].start()
+    cp_dout = pltpu.make_async_copy(dout_hbm, dout_ref, loc_s.at[16])
+    cp_dout.start()
+    cp_small = []
+    for i, (src, dst) in enumerate(
+        (
+            (act_hbm, act_ref), (atab_hbm, atab_ref), (hist_hbm, hist_ref), (gain_hbm, gain_ref),
+            (accum_hbm, accum_ref),
+        )
+    ):
+        cp_small.append(pltpu.make_async_copy(src, dst, loc_s.at[17 + i]))
+        cp_small[-1].start()
     cp_full = pltpu.make_async_copy(masters_ref, mfull, loc_s.at[1])
     cp_w = []
     for h in range(HEADS):
@@ -95,53 +113,151 @@
             )
 
     barrier = pltpu.get_barrier_semaphore()
-    for d in (1, -1):
-        pl.semaphore_signal(barrier, inc=1, device_id=(c, tab_z(d)), device_id_type=MESH)
+    for d in range(1, LEAP + 1):
+        for e in (d, -d):
+            pl.semaphore_signal(barrier, inc=1, device_id=(c, tab_z(e)), device_id_type=MESH)
     for d in range(1, Y):
         pl.semaphore_signal(barrier, inc=1, device_id=(c, tab_y(d)), device_id_type=MESH)
     for d in range(1, CTX):
         pl.semaphore_signal(barrier, inc=1, device_id=(ctx_at(d), t), device_id_type=MESH)
 
-    item = item_ref[...]
-    owner, row = lax.shift_right_logical(item, 6), item & 63
-    place = (
-        lax.shift_right_logical(owner, 2) * PLANE + ((y + Y - (owner & 3)) & 3) * ROWS + row
-    )
-    ids[c] = jnp.broadcast_to(place, (8, B))
+    for copy in cp_ids:
+        copy.wait()
+    owner, row = owner_ref[...], row_ref[...]
+    ahead = (lax.shift_right_logical(owner, 2) + Z - z) & (Z - 1)
+    slot = jnp.where(ahead > Z // 2, 2 * (Z - ahead), jnp.maximum(2 * ahead - 1, 0))
+    behind = (y + Y - (owner & (Y - 1))) & (Y - 1)
+    ids[c] = jnp.broadcast_to(behind * (Z * ROWS) + slot * ROWS + row, (8, B))
 
     cp_slice.wait()
-    tbl[z, 0:ROWS, :] = mslice[...].astype(BF16)
-    pl.semaphore_wait(barrier, CTX - 1 + Y - 1 + 2)
-
-    for d in (2, 1, 3):
-        remote(
-            tbl.at[z, pl.ds(0, ROWS)], tbl.at[z, pl.ds(d * ROWS, ROWS)],
-            y_s.at[d - 1], y_r.at[d - 1], c, tab_y(d),
-        ).start()
+    tbl[0, 0] = mslice[...].astype(BF16)
+    pl.semaphore_wait(barrier, CTX - 1 + Y - 1 + 2 * LEAP)
+
+    half_rows = (pl.ds(0, HALF), pl.ds(HALF, HALF))
+
+    def near_send(e):
+        to = SLOT_OF[-e]
+        return remote(tbl.at[0, 0], tbl.at[0, to], z_s.at[to], z_r.at[to], c, tab_z(e))
+
+    def far_send(side, f):
+        e = f if side == 0 else -f
+        src = tbl.at[0, SLOT_OF[-LEAP if side == 0 else LEAP]]
+        to = SLOT_OF[-LEAP - f if side == 0 else LEAP + f]
+        if f < LEAP:
+            return remote(src, tbl.at[0, to], z_s.at[to], z_r.at[to], c, tab_z(e))
+        at = half_rows[side]
+        return remote(
+            src.at[at], tbl.at[0, to, at], z_s.at[15 + side], z_r.at[15 + side], c, tab_z(e)
+        )
+
+    def slot_got(to):
+        if to < 15:
+            got(tbl.at[0, to], z_r.at[to], z_s.at[to])
+        else:
+            for side in range(2):
+                got(tbl.at[0, 15, half_rows[side]], z_r.at[15 + side], z_s.at[15 + side])
+
+    nearest = [e for d in range(LEAP, 0, -1) for e in (d, -d)]
+    for e in nearest:
+        near_send(e).start()
     for d in FAR_FIRST:
         remote(ids.at[c], ids.at[c], id_s.at[d - 1], id_r.at[d - 1], ctx_at(d), t).start()
 
-    def ring_send(side, k, n):
-        plane = z_at(-k) if side == 0 else z_at(k)
-        block = tbl.at[plane, pl.ds(n * PIECE, PIECE)]
+    def group_send(d, g):
+        at = pl.ds(GROUPS * g, GROUPS)
         return remote(
-            block, block, z_s.at[side, k, n], z_r.at[side, k, n], c, tab_z(1 if side == 0 else -1)
-        )
-
-    def ring_got(side, k, n):
-        plane = z_at(-1 - k) if side == 0 else z_at(1 + k)
-        got(tbl.at[plane, pl.ds(n * PIECE, PIECE)], z_r.at[side, k, n], z_s.at[side, k, n])
-
-    def far_side(n):
-        return 0 if n < CHUNKS // 2 else 1
-
-    per_piece = Y // CHUNKS
-    for n in range(CHUNKS):
-        for d in range(n * per_piece, (n + 1) * per_piece):
-            if d:
-                got(tbl.at[z, pl.ds(d * ROWS, ROWS)], y_r.at[d - 1], y_s.at[d - 1])
+            tbl.at[0, at], tbl.at[d, at], y_s.at[d - 1, g], y_r.at[d - 1, g], c, tab_y(d)
+        )
+
+    def group_got(d, g):
+        got(tbl.at[d, pl.ds(GROUPS * g, GROUPS)], y_r.at[d - 1, g], y_s.at[d - 1, g])
+
+    def sum_send(d, g):
+        return remote(
+            psum.at[d, g], yb.at[d - 1, g], ry_s.at[d - 1, g], ry_r.at[d - 1, g], c, tab_y(-d)
+        )
+
+    def sum_got(d, g):
+        got(yb.at[d - 1, g], ry_r.at[d - 1, g], ry_s.at[d - 1, g])
+
+    def gather_send(slot):
+        distance = SLOTS[slot]
+        copies = []
+        for side in range(2) if slot == 15 else (0,) if distance > 0 else (1,):
+            f = abs(distance) - LEAP
+            at = half_rows[side] if slot == 15 else pl.ds(0, ROWS)
+            copies.append(
+                remote(
+                    stage.at[slot, at], agg.at[side, f - 1, at],
+                    ag_s.at[side, f - 1], ag_r.at[side, f - 1], c, tab_z(f if side == 0 else -f),
+                )
+            )
+        return copies
+
+    def gather_got(side, f):
+        at = half_rows[side] if f == LEAP else pl.ds(0, ROWS)
+        got(agg.at[side, f - 1, at], ag_r.at[side, f - 1], ag_s.at[side, f - 1])
+
+    def target_send(slot):
+        to = SLOT_OF[-SLOTS[slot]]
+        return remote(
+            stage.at[slot], zb.at[to - 1], rz_s.at[to - 1], rz_r.at[to - 1], c, tab_z(SLOTS[slot])
+        )
+
+    def target_got(to):
+        got(zb.at[to - 1], rz_r.at[to - 1], rz_s.at[to - 1])
+
+    holder = jnp.where(c >= SPLIT, 1, 0)
+
+    def drain(upto=9):
+        for d in range(1, Y):
+            for g in range(GROUPS):
+                group_send(d, g).wait_send()
+                if upto >= 8:
+                    sum_send(d, g).wait_send()
+        for d in range(1, CTX):
+            sent(ids.at[c], id_s.at[d - 1], id_r.at[d - 1])
+            if upto >= 3:
+                sent(g1.at[0], a1_s.at[d - 1], a1_r.at[d - 1])
+            if upto >= 7:
+                sent(g2.at[0], a2_s.at[d - 1], a2_r.at[d - 1])
+            if upto >= 9:
+                sent(fin.at[c], f_s.at[d - 1], f_r.at[d - 1])
+        for e in nearest:
+            near_send(e).wait_send()
         for side in range(2):
-            ring_send(side, 0, n).start()
+            for f in range(1, LEAP + 1):
+                far_send(side, f).wait_send()
+        for slot in range(1, Z) if upto >= 8 else ():
+            for copy in gather_send(slot) if slot > 2 * LEAP else [target_send(slot)]:
+                copy.wait_send()
+        for h in range(HEADS):
+            for s in range(2):
+                need = (c <= SPLIT + REACH - 2) if s == 0 else (c >= SPLIT)
+
+                @pl.when(need & (2 * h + s != c))
+                def _():
+                    sent(dob.at[0], do_s.at[h, s], do_r.at[0])
+                    if upto >= 4:
+                        sent(stq.at[h], q_s.at[h, s], q_r.at[0])
+
+            if upto >= 4:
+                @pl.when(2 * h + holder != c)
+                def _():
+                    sent(stkv.at[h], kv_s.at[h], kv_r.at[0])
+
+        for b in range(8) if upto >= 5 else ():
+            @pl.when((c != b) & (core == (0 if b < SPLIT else 1)))
+            def _():
+                sent(dkvs.at[b], dkv_s.at[b], dkv_r.at[0])
+
+            for s in range(2):
+                need = b <= SPLIT + REACH - 2 if s == 0 else b >= SPLIT
+                if need:
+                    @pl.when((c != b) & (core == s))
+                    def _():
+                        sent(dqs.at[b], dq_s.at[b], dq_r.at[0, 0])
+                        sent(atts.at[b], at_s.at[b], at_r.at[0, 0])
 
     def to_heads(src_of, dst, ssem, rsem, local):
         for r in (2, 1, 3, 0):
@@ -164,11 +280,14 @@
     def dout_here(h):
         dob[c] = dout_ref[:, pl.ds(pl.multiple_of(h * B, B), B)]
 
+    cp_dout.wait()
     to_heads(dout_of, dob, do_s, do_r, dout_here)
     for copy in cp_w:
         copy.start()
     cp_full.start()
 
+    for copy in cp_small:
+        copy.wait()
     actb = jnp.broadcast_to(act_ref[...], (B, B)).T
     for j in range(8):
         block = pl.ds(j * B, B)
@@ -193,49 +312,64 @@
         got(ids.at[src], id_r.at[d - 1], id_s.at[d - 1])
 
     def spread(j, carry):
-        itemb[j] = jnp.broadcast_to(ids[j, 0:1, :], (B, B)).T
+        column = jnp.broadcast_to(ids[j, 0:1, :], (B, B)).T
+        at = pl.ds(8 * j, 8)
+        high[at] = lax.shift_right_logical(column, 8).astype(F32).astype(BF16).reshape(8, 16, B)
+        low[at] = (column & (PLANE - 1)).astype(F32).astype(BF16).reshape(8, 16, B)
+        line = jnp.broadcast_to(ids[j, 0:1, :], (16, B))
+        high_row[j] = lax.shift_right_logical(line, 8).astype(F32).astype(BF16)
+        low_row[j] = (line & (PLANE - 1)).astype(F32).astype(BF16)
         gacc[j] = jnp.zeros((B, B), F32)
         return carry
 
     lax.fori_loop(0, 8, spread, 0)
 
-    lane = lax.broadcasted_iota(I32, (2 * B, B), 1)
-
-    def gather_plane(plane):
-        rows = tbl[plane]
-        base = plane * PLANE
-
-        def some(i, carry):
-            at = pl.ds(2 * i, 2)
-            wanted = itemb[at].reshape(2 * B, B) - base
-            hot = jnp.concatenate(
-                [jnp.where(wanted == lane + k * B, 1.0, 0.0).astype(BF16) for k in range(2)], axis=1
-            )
-            gacc[at] = gacc[at] + dot(hot, rows).reshape(2, B, B)
-            return carry
-
-        lax.fori_loop(0, 4, some, 0)
-
-    gather_plane(z)
-
-    def ring_step(k, last):
-        for n in range(CHUNKS):
-            for side in range(2):
-                ring_got(side, k - 1, n)
-                if not last or far_side(n) == side:
-                    ring_send(side, k, n).start()
-        gather_plane(z_at(-k))
-        gather_plane(z_at(k))
-
-    def ring_body(k, carry):
-        ring_step(k, False)
-        return carry
-
-    lax.fori_loop(1, half - 1, ring_body, 0)
-    ring_step(half - 1, True)
-    for n in range(CHUNKS):
-        ring_got(far_side(n), half - 1, n)
-    gather_plane(z_at(half))
+    one, zero, none = jnp.asarray(1, BF16), jnp.asarray(0, BF16), jnp.asarray(-1, BF16)
+    lane = lax.broadcasted_iota(I32, (16, B), 1).astype(F32).astype(BF16)
+
+    def gather_tile(d, g):
+        this = jnp.asarray(d * GROUPS + g, BF16)
+        wanted = jnp.where(high[...] == this, low[...], none)
+        hot = jnp.concatenate(
+            [
+                jnp.where(wanted == (lane + jnp.asarray(k * B, BF16))[None], one, zero)
+                .reshape(8 * B, B)
+                for k in range(2)
+            ],
+            axis=1,
+        )
+        rows = tbl[d, GROUPS * g : GROUPS * (g + 1)].reshape(PLANE, B)
+        gacc[...] = gacc[...] + dot(hot, rows).reshape(8, B, B)
+
+    slot_got(SLOT_OF[-LEAP])
+    for f in range(LEAP, 0, -1):
+        far_send(0, f).start()
+    slot_got(SLOT_OF[LEAP])
+    for f in range(LEAP, 0, -1):
+        far_send(1, f).start()
+
+    def pass_on(g):
+        for to in range(GROUPS * g, GROUPS * (g + 1)):
+            if to and abs(SLOTS[to]) != LEAP:
+                slot_got(to)
+        for d in (2, 1, 3):
+            group_send(d, g).start()
+
+    pass_on(0)
+    pass_on(1)
+    gather_tile(0, 0)
+    gather_tile(0, 1)
+    for d in (1, 3, 2):
+        group_got(d, 0)
+        gather_tile(d, 0)
+    pass_on(2)
+    pass_on(3)
+    gather_tile(0, 2)
+    gather_tile(0, 3)
+    for g in (1, 2, 3):
+        for d in (1, 3, 2):
+            group_got(d, g)
+            gather_tile(d, g)
 
     for j in range(8):
         g1[j] = gacc[j].astype(BF16)
@@ -271,7 +405,6 @@
     def q_here(h):
         qb[c] = stq[h]
 
-    holder = jnp.where(c >= SPLIT, 1, 0)
     for r in (2, 1, 3, 0):
         h = lax.rem(x + r, HEADS)
         project = dot(hn[...], w_v[h])
@@ -302,14 +435,14 @@
             def _():
                 q_here(h)
 
-    def send_back(stage, ssem, rsem, dst, block):
+    def send_back(ready, ssem, rsem, dst, block):
         @pl.when(c != block)
         def _():
-            remote(stage.at[block], dst, ssem.at[block], rsem, block, t).start()
+            remote(ready.at[block], dst, ssem.at[block], rsem, block, t).start()
 
         @pl.when(c == block)
         def _():
-            dst[...] = stage[block]
+            dst[...] = ready[block]
 
     def attend(s):
         key_blocks = range(0, SPLIT) if s == 0 else range(SPLIT, 8)
@@ -425,52 +558,46 @@
         src = ctx_at(CTX - d)
         got(gin.at[src], a2_r.at[d - 1], a2_s.at[d - 1])
 
-    sub = lax.broadcasted_iota(I32, (PLANE, B), 0)
-
-    def plane_sum(plane):
-        base = plane * PLANE
+    sub = lax.broadcasted_iota(I32, (PLANE, B), 0).astype(F32).astype(BF16).reshape(16, 16, B)
+
+    def tile_sum(d, g):
+        this = jnp.asarray(d * GROUPS + g, BF16)
+        wanted = jnp.where(high_row[...] == this, low_row[...], none)
         hot = jnp.concatenate(
-            [jnp.where(ids[j, 0:1, :] - base == sub, 1.0, 0.0).astype(BF16) for j in range(8)],
+            [jnp.where(sub == wanted[j][None], one, zero).reshape(PLANE, B) for j in range(8)],
             axis=1,
         )
         return dot(hot, gin[...].reshape(8 * B, B))
 
-    def reduce_send(side, k, n):
-        at = pl.ds(n * PIECE, PIECE)
-        return remote(
-            sb.at[side, k, at], rb.at[side, k, at], rs_s.at[side, k, n], rs_r.at[side, k, n],
-            c, tab_z(1 if side == 0 else -1),
-        )
-
-    def reduce_got(side, k, n):
-        got(rb.at[side, k, pl.ds(n * PIECE, PIECE)], rs_r.at[side, k, n], rs_s.at[side, k, n])
-
-    first_sum = plane_sum(z_at(half))
-    for n in range(CHUNKS):
-        rows = slice(n * PIECE, (n + 1) * PIECE)
-        sb[far_side(n), 0, rows, :] = first_sum[rows].astype(BF16)
-        reduce_send(far_side(n), 0, n).start()
-
-    def reduce_step(k, first):
-        for side in range(2):
-            own[side] = plane_sum(z_at(half - k) if side == 0 else z_at(k - half))
-        for n in range(CHUNKS):
-            rows = slice(n * PIECE, (n + 1) * PIECE)
-            for side in range(2):
-                value = own[side, rows, :]
-                if not first or far_side(n) == side:
-                    reduce_got(side, k - 1, n)
-                    value = value + rb[side, k - 1, rows, :].astype(F32)
-                sb[side, k, rows, :] = value.astype(BF16)
-                reduce_send(side, k, n).start()
-
-    def reduce_body(k, carry):
-        reduce_step(k, False)
-        return carry
-
-    reduce_step(1, True)
-    lax.fori_loop(2, half, reduce_body, 0)
-    own[0] = plane_sum(z)
+    for g in (3, 2, 1, 0):
+        for d in (2, 1, 3):
+            psum[d, g] = tile_sum(d, g).astype(BF16)
+            sum_send(d, g).start()
+        own[g] = tile_sum(0, g)
+    for g in (3, 2, 1, 0):
+        value = own[g]
+        for d in (1, 3, 2):
+            sum_got(d, g)
+            value = value + yb[d - 1, g].astype(F32)
+        own[g] = value
+        for i in range(GROUPS):
+            slot = GROUPS * g + i
+            if slot and abs(SLOTS[slot]) != LEAP:
+                stage[slot] = value[i * ROWS : (i + 1) * ROWS].astype(BF16)
+                for copy in gather_send(slot) if slot > 2 * LEAP else [target_send(slot)]:
+                    copy.start()
+    for side in range(2):
+        slot = SLOT_OF[LEAP if side == 0 else -LEAP]
+        i = slot % GROUPS
+        total = own[slot // GROUPS, i * ROWS : (i + 1) * ROWS, :]
+        for f in range(1, LEAP):
+            gather_got(side, f)
+            total = total + agg[side, f - 1].astype(F32)
+        gather_got(side, LEAP)
+        stage[slot] = total.astype(BF16)
+        at = slice(side * HALF, (side + 1) * HALF)
+        stage[slot, at, :] = (total[at] + agg[side, LEAP - 1, at, :].astype(F32)).astype(BF16)
+        target_send(slot).start()
 
     for h in range(HEADS):
         @pl.when(2 * h + holder != c)
@@ -489,23 +616,10 @@
 
         att_out[:, h * B : (h + 1) * B] = dqf[...].astype(BF16)
 
-    for n in range(CHUNKS):
-        rows = slice(n * PIECE, (n + 1) * PIECE)
-        value = own[0, rows, :]
-        for side in range(2):
-            reduce_got(side, half - 1, n)
-            value = value + rb[side, half - 1, rows, :].astype(F32)
-        own[0, rows, :] = value
-
-    for d in (2, 1, 3):
-        yb[0, d - 1] = own[0, d * ROWS : (d + 1) * ROWS, :].astype(BF16)
-        remote(
-            yb.at[0, d - 1], yb.at[1, d - 1], ry_s.at[d - 1], ry_r.at[d - 1], c, tab_y(-d)
-        ).start()
     value = own[0, 0:ROWS, :]
-    for d in (1, 3, 2):
-        got(yb.at[1, d - 1], ry_r.at[d - 1], ry_s.at[d - 1])
-        value = value + yb[1, d - 1].astype(F32)
+    for to in range(1, 2 * LEAP + 1):
+        target_got(to)
+        value = value + zb[to - 1].astype(F32)
 
     fin[c] = value.astype(BF16)
     for d in FAR_FIRST:
@@ -531,70 +645,38 @@
         cols = slice(j * B, (j + 1) * B)
         nm_out[:, cols] = mfull[:, cols] - fin[j].astype(F32) * rate
 
-    for d in range(1, Y):
-        sent(tbl.at[z, pl.ds(0, ROWS)], y_s.at[d - 1], y_r.at[d - 1])
-        sent(yb.at[0, d - 1], ry_s.at[d - 1], ry_r.at[d - 1])
-    for d in range(1, CTX):
-        sent(ids.at[c], id_s.at[d - 1], id_r.at[d - 1])
-        sent(g1.at[0], a1_s.at[d - 1], a1_r.at[d - 1])
-        sent(g2.at[0], a2_s.at[d - 1], a2_r.at[d - 1])
-        sent(fin.at[c], f_s.at[d - 1], f_r.at[d - 1])
-    for side in range(2):
-        for n in range(CHUNKS):
-            for k in range(half):
-                if k < half - 1 or far_side(n) == side:
-                    ring_send(side, k, n).wait_send()
-                if k > 0 or far_side(n) == side:
-                    reduce_send(side, k, n).wait_send()
-    for h in range(HEADS):
-        @pl.when(2 * h + holder != c)
-        def _():
-            sent(stkv.at[h], kv_s.at[h], kv_r.at[0])
-
-        for s in range(2):
-            need = (c <= SPLIT + REACH - 2) if s == 0 else (c >= SPLIT)
-
-            @pl.when(need & (2 * h + s != c))
-            def _():
-                sent(stq.at[h], q_s.at[h, s], q_r.at[0])
-                sent(dob.at[0], do_s.at[h, s], do_r.at[0])
-
-    for b in range(8):
-        @pl.when((c != b) & (core == (0 if b < SPLIT else 1)))
-        def _():
-            sent(dkvs.at[b], dkv_s.at[b], dkv_r.at[0])
-
-        for s in range(2):
-            need = b <= SPLIT + REACH - 2 if s == 0 else b >= SPLIT
-            if need:
-                @pl.when((c != b) & (core == s))
-                def _():
-                    sent(dqs.at[b], dq_s.at[b], dq_r.at[0, 0])
-                    sent(atts.at[b], at_s.at[b], at_r.at[0, 0])
+    drain()
 
 
 def per_device(
     item_owner, item_row, action_id, history_len, masters, row_accum, action_table, norm_gain,
     w_qkv, d_attended,
 ):
-    planes = lax.axis_size("tab") // Y
-    half = planes // 2
-    item = item_owner[0, :, 0][None, :] * ROWS + item_row
     vmem = pl.BlockSpec(memory_space=pltpu.VMEM)
-    smem = pl.BlockSpec(memory_space=pltpu.SMEM)
-    hbm = pl.BlockSpec(memory_space=pl.ANY)
+    hbm = pl.BlockSpec(memory_space=pltpu.HBM)
     dma = pltpu.SemaphoreType.DMA
 
     def block(*lead, rows=B, cols=B, dtype=BF16):
         return pltpu.VMEM((*lead, rows, cols), dtype)
 
     scratch = [
+        pltpu.VMEM((1, B), I32),
+        pltpu.VMEM((1, B), I32),
+        pltpu.VMEM((1, B), I32),
+        pltpu.SMEM((1, 4), I32),
+        pltpu.VMEM((1, ROWS), F32),
+        pltpu.VMEM((8, MODEL), F32),
+        pltpu.VMEM((1, MODEL), F32),
+        pltpu.VMEM((B, HEADS * B), BF16),
         pltpu.VMEM((ROWS, B), F32),
         pltpu.VMEM((ROWS, MODEL), F32),
         pltpu.VMEM((HEADS, MODEL, 3 * B), BF16),
-        block(planes, rows=PLANE),
+        block(Y, Z, rows=ROWS),
         block(8, rows=8, dtype=I32),
-        block(8, dtype=I32),
+        block(HEADS * 16, rows=16),
+        block(HEADS * 16, rows=16),
+        block(8, rows=16),
+        block(8, rows=16),
         block(8, dtype=F32),
         block(8),
         block(8),
@@ -620,14 +702,16 @@
         block(cols=MODEL, dtype=F32),
         block(8),
         block(8),
-        block(2, half, rows=PLANE),
-        block(2, half, rows=PLANE),
-        block(2, rows=PLANE, dtype=F32),
-        block(2, Y - 1, rows=ROWS),
+        block(Y, GROUPS, rows=PLANE),
+        block(GROUPS, rows=PLANE, dtype=F32),
+        block(Y - 1, GROUPS, rows=PLANE),
+        block(Z, rows=ROWS),
+        block(2, LEAP, rows=ROWS),
+        block(2 * LEAP, rows=ROWS),
         block(8, rows=ROWS),
-        dma((14,)),
-        dma((Y - 1,)), dma((Y - 1,)),
-        dma((2, half, CHUNKS)), dma((2, half, CHUNKS)),
+        dma((22,)),
+        dma((Y - 1, GROUPS)), dma((Y - 1, GROUPS)),
+        dma((Z + 1,)), dma((Z + 1,)),
         dma((7,)), dma((7,)),
         dma((7,)), dma((7,)),
         dma((HEADS, 2)), dma((8,)),
@@ -637,26 +721,27 @@
         dma((8,)), dma((HEADS,)),
         dma((8,)), dma((2, HEADS)),
         dma((7,)), dma((7,)),
-        dma((2, half, CHUNKS)), dma((2, half, CHUNKS)),
-        dma((Y - 1,)), dma((Y - 1,)),
+        dma((Y - 1, GROUPS)), dma((Y - 1, GROUPS)),
+        dma((2, LEAP)), dma((2, LEAP)),
+        dma((2 * LEAP,)), dma((2 * LEAP,)),
         dma((7,)), dma((7,)),
     ]
     attended, row_grads, new_masters, new_accum = pl.pallas_call(
-        functools.partial(kernel, planes),
+        kernel,
         out_shape=(
             jax.ShapeDtypeStruct((B, HEADS * B), BF16),
             jax.ShapeDtypeStruct((ROWS, MODEL), F32),
             jax.ShapeDtypeStruct((ROWS, MODEL), F32),
             jax.ShapeDtypeStruct((1, ROWS), F32),
         ),
-        in_specs=[vmem, vmem, smem, hbm, vmem, vmem, vmem, hbm, vmem],
+        in_specs=[hbm] * 10,
         out_specs=(vmem, vmem, vmem, vmem),
         scratch_shapes=scratch,
         compiler_params=pltpu.CompilerParams(
-            collective_id=0, has_side_effects=True, vmem_limit_bytes=48 * 1024 * 1024
+            collective_id=0, has_side_effects=True, vmem_limit_bytes=63 * 1024 * 1024
         ),
     )(
-        item, action_id, history_len, masters, row_accum[None, :], action_table,
+        item_owner[:, :, 0], item_row, action_id, history_len, masters, row_accum[None, :], action_table,
         norm_gain[None, :], w_qkv, d_attended[0],
     )
     return (attended[None], row_grads, new_masters, new_accum[0])

time: 123 us -> 96.3 us (0.78)
  Pallas kernels: 112 us -> 89.3 us
  local copies, waits for them, and re-layouts: 9.72 us -> 6.08 us
    pallas_call x1, Pallas kernels: 112 us -> 89.3 us  [per_device(): pl.pallas_call(kernel, out_shape=(jax.ShapeDtypeStruct((B, HEADS * B), BF...]
    unnamed x20 -> x4, local copies, waits for them, and re-layouts: 9.72 us -> 6.08 us
where the time goes in v2:
time: 96.3 us; the launch traced here: 96 us
  Pallas kernels  89.3 us (93%)
  local copies, waits for them, and re-layouts  6.08 us (6%)
    pallas_call x1, Pallas kernels, per_device(): pl.pallas_call(kernel, out_shape=(jax.ShapeDtypeStruct((B, HEADS * B), BF...  89.3 us
    unnamed x4, local copies, waits for them, and re-layouts  6.08 us

profile of v2, /device:TPU:1, one launch (start us, length us, event | category | flops | bytes accessed | tf_op | source)
XLA Modules:
  0.0 96.0 jit_solution(10081137424842756754)
XLA Ops:
  0.6 89.3 %shard_map.129 = (bf16[128,512]{1,0:T(8,128)(2,1)}, f32[64,1024]{1,0:T(8,128)}, f32[64,1024]{1,0:T(8,128)}, f32[1,64]{1,0:T(1,128)}) custom-call(s32[1,128]{1,0:T(1,128)} %bitcast.9, s32[1,128]{1,0:T(1,128)} %row_hbm.1, s32[1,128]{1,0:T(1,128)} %act_hbm.1, s32[1,4]{1,0:T(1,128)} %hist_hbm.1, f32[64,1024]{1,0:T(8,128)} %masters_ref.1, f32[1,64]{1,0:T(1,128)} %bitcast.10, ...), custom_call_target="tpu_custom_call" | custom-call | tf_op jit(solution)/shard_map/pallas_call | solution.py:729
  90.0 1.6 %copy.18 = bf16[1,128,512]{2,1,0:T(8,128)(2,1)} copy(bf16[1,128,512]{2,1,0:T(8,128)(2,1)} %bitcast.6) | data formatting | bytes 262144
  91.5 1.7 %copy.19 = f32[64,1024]{1,0:T(8,128)} copy(f32[64,1024]{1,0:T(8,128)} %get-tuple-element.17) | data formatting | bytes 524288
  93.2 1.7 %copy.20 = f32[64,1024]{1,0:T(8,128)} copy(f32[64,1024]{1,0:T(8,128)} %get-tuple-element.18) | data formatting | bytes 524288
  94.9 1.2 %copy.21 = f32[64]{0:T(128)} copy(f32[64]{0:T(128)} %bitcast.11) | data formatting | bytes 512

commit v3 on v2

--- a/solution.py
+++ b/solution.py
@@ -28,6 +28,7 @@
 SLOT_OF = {distance: slot for slot, distance in enumerate(SLOTS)} | {-8: 15}
 LEAP = 4
 HALF = ROWS // 2
+VMEM_BYTES = 63 * 1024 * 1024
 SPLIT = 3
 REACH = 5
 SCALE = 1.0 / math.sqrt(B)
@@ -37,16 +38,20 @@
 TN = (((0,), (0,)), ((), ()))
 
 
+def sigmoid(value):
+    return 0.5 * jnp.tanh(0.5 * value) + 0.5
+
+
 def dot(a, b, dims=(((1,), (0,)), ((), ()))):
     return lax.dot_general(a, b, dims, preferred_element_type=F32)
 
 
 def kernel(
-    owner_hbm, row_hbm, act_hbm, hist_hbm, masters_ref, accum_hbm, atab_hbm, gain_hbm, w_ref,
+    owner_hbm, row_hbm, act_hbm, hist_hbm, masters_ref, atab_hbm, gain_hbm, w_ref,
     dout_hbm,
-    att_out, rg_out, nm_out, na_out,
-    owner_ref, row_ref, act_ref, hist_ref, accum_ref, atab_ref, gain_ref, dout_ref,
-    mslice, mfull, w_v, tbl, ids, high, low, high_row, low_row, gacc, g1, x1, xin, hn, startb, invb,
+    att_out, grad_out,
+    owner_ref, row_ref, act_ref, hist_ref, atab_ref, gain_ref, dout_ref,
+    mslice, w_v, tbl, ids, high, low, high_row, low_row, gacc, g1, x1, xin, hn, startb, invb,
     pd, stq, stkv, qb, kvb, dob, attacc, dqacc, dqs, dkvs, atts, rdq, rdkv, ratt, dqf, gh,
     g2, gin, psum, own, yb, stage, agg, zb, fin,
     loc_s, y_s, y_r, z_s, z_r, id_s, id_r, a1_s, a1_r, q_s, q_r, kv_s, kv_r, do_s, do_r,
@@ -95,12 +100,10 @@
     for i, (src, dst) in enumerate(
         (
             (act_hbm, act_ref), (atab_hbm, atab_ref), (hist_hbm, hist_ref), (gain_hbm, gain_ref),
-            (accum_hbm, accum_ref),
         )
     ):
         cp_small.append(pltpu.make_async_copy(src, dst, loc_s.at[17 + i]))
         cp_small[-1].start()
-    cp_full = pltpu.make_async_copy(masters_ref, mfull, loc_s.at[1])
     cp_w = []
     for h in range(HEADS):
         for part in range(3):
@@ -121,14 +124,6 @@
     for d in range(1, CTX):
         pl.semaphore_signal(barrier, inc=1, device_id=(ctx_at(d), t), device_id_type=MESH)
 
-    for copy in cp_ids:
-        copy.wait()
-    owner, row = owner_ref[...], row_ref[...]
-    ahead = (lax.shift_right_logical(owner, 2) + Z - z) & (Z - 1)
-    slot = jnp.where(ahead > Z // 2, 2 * (Z - ahead), jnp.maximum(2 * ahead - 1, 0))
-    behind = (y + Y - (owner & (Y - 1))) & (Y - 1)
-    ids[c] = jnp.broadcast_to(behind * (Z * ROWS) + slot * ROWS + row, (8, B))
-
     cp_slice.wait()
     tbl[0, 0] = mslice[...].astype(BF16)
     pl.semaphore_wait(barrier, CTX - 1 + Y - 1 + 2 * LEAP)
@@ -160,6 +155,14 @@
     nearest = [e for d in range(LEAP, 0, -1) for e in (d, -d)]
     for e in nearest:
         near_send(e).start()
+    for copy in cp_ids:
+        copy.wait()
+    owner, row = owner_ref[...], row_ref[...]
+    ahead = (lax.shift_right_logical(owner, 2) + Z - z) & (Z - 1)
+    slot = jnp.where(ahead > Z // 2, 2 * (Z - ahead), jnp.maximum(2 * ahead - 1, 0))
+    behind = (y + Y - (owner & (Y - 1))) & (Y - 1)
+    ids[c] = jnp.broadcast_to(behind * (Z * ROWS) + slot * ROWS + row, (8, B))
+
     for d in FAR_FIRST:
         remote(ids.at[c], ids.at[c], id_s.at[d - 1], id_r.at[d - 1], ctx_at(d), t).start()
 
@@ -284,7 +287,6 @@
     to_heads(dout_of, dob, do_s, do_r, dout_here)
     for copy in cp_w:
         copy.start()
-    cp_full.start()
 
     for copy in cp_small:
         copy.wait()
@@ -408,7 +410,7 @@
     for r in (2, 1, 3, 0):
         h = lax.rem(x + r, HEADS)
         project = dot(hn[...], w_v[h])
-        sig = jax.nn.sigmoid(project)
+        sig = sigmoid(project)
         pd[h] = sig * (1.0 + project * (1.0 - sig))
         active = (project * sig).astype(BF16)
         stq[h] = active[:, 0:B]
@@ -447,7 +449,6 @@
     def attend(s):
         key_blocks = range(0, SPLIT) if s == 0 else range(SPLIT, 8)
         lowest = key_blocks[0]
-        query_blocks = range(0, SPLIT + REACH - 1) if s == 0 else range(SPLIT, 8)
         waited = set()
         for kb in key_blocks:
             end = min(kb + REACH, 8)
@@ -467,21 +468,21 @@
                         got(dob.at[b], do_r.at[b], do_s.at[0, 0])
 
             queries = qb[kb:end].reshape(n, B)
-            grad_out = dob[kb:end].reshape(n, B)
+            cotangent = dob[kb:end].reshape(n, B)
             keys = kvb[kb, :, 0:B]
             values = kvb[kb, :, B : 2 * B]
             raw = dot(queries, keys, NT) * SCALE
-            sig = jax.nn.sigmoid(raw)
+            sig = sigmoid(raw)
             inv = invb[kb:end].reshape(n, B)
             k_pos = lax.broadcasted_iota(I32, (n, B), 1) + kb * B
             q_pos = lax.broadcasted_iota(I32, (n, B), 0) + kb * B
             allowed = (k_pos >= startb[kb:end].reshape(n, B)) & (k_pos <= q_pos)
             weights = jnp.where(allowed, raw * sig * inv, 0.0).astype(BF16)
-            grad_w = dot(grad_out, values, NT)
+            grad_w = dot(cotangent, values, NT)
             slope = sig * (1.0 + raw * (1.0 - sig))
             grad_raw = jnp.where(allowed, grad_w * slope * (inv * SCALE), 0.0).astype(BF16)
             dkvs[kb, :, 0:B] = dot(grad_raw, queries, TN).astype(BF16)
-            dkvs[kb, :, B : 2 * B] = dot(weights, grad_out, TN).astype(BF16)
+            dkvs[kb, :, B : 2 * B] = dot(weights, cotangent, TN).astype(BF16)
             send_back(dkvs, dkv_s, dkv_r.at[x], rdkv.at[x], kb)
             dq = dot(grad_raw, keys)
             at = dot(weights, values)
@@ -498,8 +499,6 @@
                 else:
                     dqacc[b] = dq_b
                     attacc[b] = at_b
-        for b in query_blocks:
-            send_back(atts, at_s, at_r.at[s, x], ratt.at[s, x], b)
 
     for s in range(2):
         @pl.when(core == s)
@@ -557,6 +556,12 @@
     for d in range(1, CTX):
         src = ctx_at(CTX - d)
         got(gin.at[src], a2_r.at[d - 1], a2_s.at[d - 1])
+
+    for s in range(2):
+        @pl.when(core == s)
+        def _():
+            for b in range(0, SPLIT + REACH - 1) if s == 0 else range(SPLIT, 8):
+                send_back(atts, at_s, at_r.at[s, x], ratt.at[s, x], b)
 
     sub = lax.broadcasted_iota(I32, (PLANE, B), 0).astype(F32).astype(BF16).reshape(16, 16, B)
 
@@ -624,28 +629,54 @@
     fin[c] = value.astype(BF16)
     for d in FAR_FIRST:
         remote(fin.at[c], fin.at[c], f_s.at[d - 1], f_r.at[d - 1], ctx_at(d), t).start()
-    cp_full.wait()
     for d in range(1, CTX):
         src = ctx_at(CTX - d)
         got(fin.at[src], f_r.at[d - 1], f_s.at[d - 1])
 
+    grad_out[...] = fin[...]
+    drain()
+
+
+def adagrad(
+    grad_hbm, att_hbm, masters_hbm, accum_hbm, att_out, rg_out, nm_out, na_out,
+    grad, rows, accum, rg, nm, na, sem,
+):
+    copies = [
+        pltpu.make_async_copy(src, dst, sem.at[i])
+        for i, (src, dst) in enumerate(
+            ((grad_hbm, grad), (masters_hbm, rows), (accum_hbm, accum), (att_hbm, att_out))
+        )
+    ]
+    for copy in copies:
+        copy.start()
+    copies[0].wait()
     total = jnp.zeros((ROWS, B), F32)
     for j in range(8):
-        g = fin[j].astype(F32)
-        rg_out[:, j * B : (j + 1) * B] = g
+        g = grad[j].astype(F32)
+        rg[:, j * B : (j + 1) * B] = g
         total = total + g * g
+    results = [
+        pltpu.make_async_copy(src, dst, sem.at[4 + i])
+        for i, (src, dst) in enumerate(((rg, rg_out), (nm, nm_out), (na, na_out)))
+    ]
+    results[0].start()
+    copies[2].wait()
     diagonal = lax.broadcasted_iota(I32, (ROWS, ROWS), 0) == lax.broadcasted_iota(
         I32, (ROWS, ROWS), 1
     )
-    before = jnp.sum(jnp.where(diagonal, accum_ref[...], 0.0), axis=1, keepdims=True)
+    before = jnp.sum(jnp.where(diagonal, accum[...], 0.0), axis=1, keepdims=True)
     after = before + jnp.sum(total, axis=1, keepdims=True) * (1.0 / MODEL)
-    na_out[...] = jnp.sum(jnp.where(diagonal, after, 0.0), axis=0, keepdims=True)
     rate = LEARN_RATE * lax.rsqrt(after)
+    copies[1].wait()
     for j in range(8):
         cols = slice(j * B, (j + 1) * B)
-        nm_out[:, cols] = mfull[:, cols] - fin[j].astype(F32) * rate
-
-    drain()
+        nm[:, cols] = rows[:, cols] - rg[:, cols] * rate
+    results[1].start()
+    na[...] = jnp.sum(jnp.where(diagonal, after, 0.0), axis=0, keepdims=True)
+    results[2].start()
+    copies[3].wait()
+    for copy in results:
+        copy.wait()
 
 
 def per_device(
@@ -664,12 +695,10 @@
         pltpu.VMEM((1, B), I32),
         pltpu.VMEM((1, B), I32),
         pltpu.SMEM((1, 4), I32),
-        pltpu.VMEM((1, ROWS), F32),
         pltpu.VMEM((8, MODEL), F32),
         pltpu.VMEM((1, MODEL), F32),
         pltpu.VMEM((B, HEADS * B), BF16),
         pltpu.VMEM((ROWS, B), F32),
-        pltpu.VMEM((ROWS, MODEL), F32),
         pltpu.VMEM((HEADS, MODEL, 3 * B), BF16),
         block(Y, Z, rows=ROWS),
         block(8, rows=8, dtype=I32),
@@ -726,24 +755,43 @@
         dma((2 * LEAP,)), dma((2 * LEAP,)),
         dma((7,)), dma((7,)),
     ]
+    attended, grads = pl.pallas_call(
+        kernel,
+        out_shape=(
+            jax.ShapeDtypeStruct((B, HEADS * B), BF16),
+            jax.ShapeDtypeStruct((8, ROWS, B), BF16),
+        ),
+        in_specs=[hbm] * 9,
+        out_specs=(vmem, vmem),
+        scratch_shapes=scratch,
+        compiler_params=pltpu.CompilerParams(
+            collective_id=0, has_side_effects=True, vmem_limit_bytes=VMEM_BYTES
+        ),
+    )(
+        item_owner[:, :, 0], item_row, action_id, history_len, masters, action_table,
+        norm_gain[None, :], w_qkv, d_attended[0],
+    )
     attended, row_grads, new_masters, new_accum = pl.pallas_call(
-        kernel,
+        adagrad,
         out_shape=(
             jax.ShapeDtypeStruct((B, HEADS * B), BF16),
             jax.ShapeDtypeStruct((ROWS, MODEL), F32),
             jax.ShapeDtypeStruct((ROWS, MODEL), F32),
             jax.ShapeDtypeStruct((1, ROWS), F32),
         ),
-        in_specs=[hbm] * 10,
-        out_specs=(vmem, vmem, vmem, vmem),
-        scratch_shapes=scratch,
-        compiler_params=pltpu.CompilerParams(
-            collective_id=0, has_side_effects=True, vmem_limit_bytes=63 * 1024 * 1024
-        ),
-    )(
-        item_owner[:, :, 0], item_row, action_id, history_len, masters, row_accum[None, :], action_table,
-        norm_gain[None, :], w_qkv, d_attended[0],
-    )
+        in_specs=[hbm] * 4,
+        out_specs=(hbm, hbm, hbm, hbm),
+        scratch_shapes=[
+            block(8, rows=ROWS),
+            pltpu.VMEM((ROWS, MODEL), F32),
+            pltpu.VMEM((1, ROWS), F32),
+            pltpu.VMEM((ROWS, MODEL), F32),
+            pltpu.VMEM((ROWS, MODEL), F32),
+            pltpu.VMEM((1, ROWS), F32),
+            dma((7,)),
+        ],
+        compiler_params=pltpu.CompilerParams(vmem_limit_bytes=VMEM_BYTES),
+    )(grads, attended, masters, row_accum[None, :])
     return (attended[None], row_grads, new_masters, new_accum[0])
 
 

time: 96.3 us -> 94.7 us (0.983)
  local copies, waits for them, and re-layouts: 6.08 us -> 0 us
  Pallas kernels: 89.3 us -> 93.7 us
    unnamed x4 -> x0, local copies, waits for them, and re-layouts: 6.08 us -> none
    pallas_call x0 -> x1, Pallas kernels: none -> 5.14 us  [per_device(): pl.pallas_call(adagrad, out_shape=(jax.ShapeDtypeStruct((B, HEADS * B), B...]
where the time goes in v3:
time: 94.7 us; the launch traced here: 94.5 us
  Pallas kernels  93.7 us (99%)
    pallas_call x1, Pallas kernels, per_device(): pl.pallas_call(kernel, out_shape=(jax.ShapeDtypeStruct((B, HEADS * B), BF...  88.6 us
    pallas_call x1, Pallas kernels, per_device(): pl.pallas_call(adagrad, out_shape=(jax.ShapeDtypeStruct((B, HEADS * B), B...  5.14 us

profile of v3, /device:TPU:1, one launch (start us, length us, event | category | flops | bytes accessed | tf_op | source)
XLA Modules:
  0.0 94.5 jit_solution(12942059627711336983)
XLA Ops:
  0.6 88.6 %shard_map.129 = (bf16[128,512]{1,0:T(8,128)(2,1)}, bf16[8,64,128]{2,1,0:T(8,128)(2,1)}) custom-call(s32[1,128]{1,0:T(1,128)} %bitcast.9, s32[1,128]{1,0:T(1,128)} %row_hbm.1, s32[1,128]{1,0:T(1,128)} %act_hbm.1, s32[1,4]{1,0:T(1,128)} %hist_hbm.1, f32[64,1024]{1,0:T(8,128)} %masters_hbm.1, f32[8,1024]{1,0:T(8,128)} %atab_hbm.1, f32[1,1024]{1,0:T(1,128)} %bitcast.7, ...), custom_call_target="tpu_custom_call" | custom-call | tf_op jit(solution)/shard_map/pallas_call | solution.py:758
  89.2 5.1 %shard_map.130 = (bf16[128,512]{1,0:T(8,128)(2,1)}, f32[64,1024]{1,0:T(8,128)}, f32[64,1024]{1,0:T(8,128)}, f32[1,64]{1,0:T(1,128)}) custom-call(bf16[8,64,128]{2,1,0:T(8,128)(2,1)} %get-tuple-element.10.grad_hbm, bf16[128,512]{1,0:T(8,128)(2,1)} %get-tuple-element.11.att_hbm, f32[64,1024]{1,0:T(8,128)} %masters_hbm.1, f32[1,64]{1,0:T(1,128)} %bitcast.8), custom_call_target="tpu_custom_call" | custom-call | tf_op jit(solution)/shard_map/pallas_call | solution.py:774

commit v4 on v3

--- a/solution.py
+++ b/solution.py
@@ -28,6 +28,7 @@
 SLOT_OF = {distance: slot for slot, distance in enumerate(SLOTS)} | {-8: 15}
 LEAP = 4
 HALF = ROWS // 2
+ASKED = 64
 VMEM_BYTES = 63 * 1024 * 1024
 SPLIT = 3
 REACH = 5
@@ -51,10 +52,11 @@
     dout_hbm,
     att_out, grad_out,
     owner_ref, row_ref, act_ref, hist_ref, atab_ref, gain_ref, dout_ref,
-    mslice, w_v, tbl, ids, high, low, high_row, low_row, gacc, g1, x1, xin, hn, startb, invb,
+    mslice, w_v, tbl, ids, high, low, high_row, low_row, unpack, wish_out, wishes,
+    gacc, picked, x1, xin, hn, startb, invb,
     pd, stq, stkv, qb, kvb, dob, attacc, dqacc, dqs, dkvs, atts, rdq, rdkv, ratt, dqf, gh,
     g2, gin, psum, own, yb, stage, agg, zb, fin,
-    loc_s, y_s, y_r, z_s, z_r, id_s, id_r, a1_s, a1_r, q_s, q_r, kv_s, kv_r, do_s, do_r,
+    loc_s, w_s, w_r, z_s, z_r, id_s, id_r, a1_s, a1_r, q_s, q_r, kv_s, kv_r, do_s, do_r,
     dq_s, dq_r, dkv_s, dkv_r, at_s, at_r, a2_s, a2_r, ry_s, ry_r, ag_s, ag_r, rz_s, rz_r, f_s, f_r,
 ):
     c = lax.axis_index("ctx")
@@ -119,38 +121,40 @@
     for d in range(1, LEAP + 1):
         for e in (d, -d):
             pl.semaphore_signal(barrier, inc=1, device_id=(c, tab_z(e)), device_id_type=MESH)
-    for d in range(1, Y):
-        pl.semaphore_signal(barrier, inc=1, device_id=(c, tab_y(d)), device_id_type=MESH)
-    for d in range(1, CTX):
-        pl.semaphore_signal(barrier, inc=1, device_id=(ctx_at(d), t), device_id_type=MESH)
+    for e in range(Y):
+        for d in range(CTX):
+            if e or d:
+                pl.semaphore_signal(
+                    barrier, inc=1, device_id=(ctx_at(d), tab_y(e)), device_id_type=MESH
+                )
 
     cp_slice.wait()
-    tbl[0, 0] = mslice[...].astype(BF16)
-    pl.semaphore_wait(barrier, CTX - 1 + Y - 1 + 2 * LEAP)
+    tbl[0] = mslice[...].astype(BF16)
+    pl.semaphore_wait(barrier, Y * CTX - 1 + 2 * LEAP)
 
     half_rows = (pl.ds(0, HALF), pl.ds(HALF, HALF))
 
     def near_send(e):
         to = SLOT_OF[-e]
-        return remote(tbl.at[0, 0], tbl.at[0, to], z_s.at[to], z_r.at[to], c, tab_z(e))
+        return remote(tbl.at[0], tbl.at[to], z_s.at[to], z_r.at[to], c, tab_z(e))
 
     def far_send(side, f):
         e = f if side == 0 else -f
-        src = tbl.at[0, SLOT_OF[-LEAP if side == 0 else LEAP]]
+        src = tbl.at[SLOT_OF[-LEAP if side == 0 else LEAP]]
         to = SLOT_OF[-LEAP - f if side == 0 else LEAP + f]
         if f < LEAP:
-            return remote(src, tbl.at[0, to], z_s.at[to], z_r.at[to], c, tab_z(e))
+            return remote(src, tbl.at[to], z_s.at[to], z_r.at[to], c, tab_z(e))
         at = half_rows[side]
         return remote(
-            src.at[at], tbl.at[0, to, at], z_s.at[15 + side], z_r.at[15 + side], c, tab_z(e)
+            src.at[at], tbl.at[to, at], z_s.at[15 + side], z_r.at[15 + side], c, tab_z(e)
         )
 
     def slot_got(to):
         if to < 15:
-            got(tbl.at[0, to], z_r.at[to], z_s.at[to])
+            got(tbl.at[to], z_r.at[to], z_s.at[to])
         else:
             for side in range(2):
-                got(tbl.at[0, 15, half_rows[side]], z_r.at[15 + side], z_s.at[15 + side])
+                got(tbl.at[15, half_rows[side]], z_r.at[15 + side], z_s.at[15 + side])
 
     nearest = [e for d in range(LEAP, 0, -1) for e in (d, -d)]
     for e in nearest:
@@ -160,20 +164,52 @@
     owner, row = owner_ref[...], row_ref[...]
     ahead = (lax.shift_right_logical(owner, 2) + Z - z) & (Z - 1)
     slot = jnp.where(ahead > Z // 2, 2 * (Z - ahead), jnp.maximum(2 * ahead - 1, 0))
-    behind = (y + Y - (owner & (Y - 1))) & (Y - 1)
-    ids[c] = jnp.broadcast_to(behind * (Z * ROWS) + slot * ROWS + row, (8, B))
-
+    asked = slot * ROWS + row
+    owner_y = owner & (Y - 1)
+    behind = (y + Y - owner_y) & (Y - 1)
+    ids[c] = jnp.broadcast_to(behind * (Z * ROWS) + asked, (8, B))
+
+    lane = lax.broadcasted_iota(I32, (B, B), 1)
+    sub = lax.broadcasted_iota(I32, (B, B), 0)
+    column = jnp.broadcast_to(owner_y * (Z * ROWS) + asked, (B, B)).T
+    column_y = lax.shift_right_logical(column, 10)
+    asked_of = (column & (Z * ROWS - 1)).astype(F32) + 1.0
+    earlier = (column_y == jnp.broadcast_to(owner_y, (B, B))) & (lane < sub)
+    rank = jnp.sum(jnp.where(earlier, 1.0, 0.0), axis=1, keepdims=True)
+    pos = column_y * ASKED + jnp.broadcast_to(rank, (B, B)).astype(I32)
+    for k in range(2):
+        unpack[:, k * B : (k + 1) * B] = jnp.where(pos == lane + k * B, 1.0, 0.0).astype(BF16)
+    number = lane - core * ASKED
+    valid = (number >= 0) & (number < ASKED)
+    for e in range(Y):
+        mine = valid & (pos == number + ((y + Y - e) & (Y - 1)) * ASKED)
+        wish = jnp.sum(jnp.where(mine, asked_of, 0.0), axis=0, keepdims=True)
+        wish_out[e] = jnp.broadcast_to(wish, (8, B))
+
+    def wish_send(e, d):
+        return remote(
+            wish_out.at[e], wishes.at[e, c], w_s.at[e, d], w_r.at[e, c], ctx_at(d), tab_y(-e)
+        )
+
+    for e in (2, 1, 3, 0):
+        for d in FAR_FIRST + ((0,) if e else ()):
+            wish_send(e, d).start()
+    wishes[0, c] = wish_out[0]
     for d in FAR_FIRST:
         remote(ids.at[c], ids.at[c], id_s.at[d - 1], id_r.at[d - 1], ctx_at(d), t).start()
 
-    def group_send(d, g):
-        at = pl.ds(GROUPS * g, GROUPS)
+    def row_send(e, d):
+        to = ctx_at(d)
+        at = pl.ds(pl.multiple_of(lax.rem(to, 2) * ASKED, ASKED), ASKED)
         return remote(
-            tbl.at[0, at], tbl.at[d, at], y_s.at[d - 1, g], y_r.at[d - 1, g], c, tab_y(d)
-        )
-
-    def group_got(d, g):
-        got(tbl.at[d, pl.ds(GROUPS * g, GROUPS)], y_r.at[d - 1, g], y_s.at[d - 1, g])
+            picked.at[e * 4 + lax.div(to, 2), at],
+            x1.at[c, pl.ds(pl.multiple_of(y * ASKED, ASKED), ASKED)],
+            a1_s.at[e, d], a1_r.at[e, c], to, tab_y(e),
+        )
+
+    def row_got(e, src):
+        at = pl.ds(pl.multiple_of(((y + Y - e) & (Y - 1)) * ASKED, ASKED), ASKED)
+        got(x1.at[src, at], a1_r.at[e, src], a1_s.at[0, 0])
 
     def sum_send(d, g):
         return remote(
@@ -215,19 +251,22 @@
     def drain(upto=9):
         for d in range(1, Y):
             for g in range(GROUPS):
-                group_send(d, g).wait_send()
                 if upto >= 8:
                     sum_send(d, g).wait_send()
         for d in range(1, CTX):
             sent(ids.at[c], id_s.at[d - 1], id_r.at[d - 1])
-            if upto >= 3:
-                sent(g1.at[0], a1_s.at[d - 1], a1_r.at[d - 1])
             if upto >= 7:
                 sent(g2.at[0], a2_s.at[d - 1], a2_r.at[d - 1])
             if upto >= 9:
                 sent(fin.at[c], f_s.at[d - 1], f_r.at[d - 1])
         for e in nearest:
             near_send(e).wait_send()
+        for e in range(Y):
+            for d in range(CTX):
+                if e or d:
+                    wish_send(e, d).wait_send()
+                    if upto >= 3:
+                        row_send(e, d).wait_send()
         for side in range(2):
             for f in range(1, LEAP + 1):
                 far_send(side, f).wait_send()
@@ -287,6 +326,13 @@
     to_heads(dout_of, dob, do_s, do_r, dout_here)
     for copy in cp_w:
         copy.start()
+
+    slot_got(SLOT_OF[-LEAP])
+    for f in range(LEAP, 0, -1):
+        far_send(0, f).start()
+    slot_got(SLOT_OF[LEAP])
+    for f in range(LEAP, 0, -1):
+        far_send(1, f).start()
 
     for copy in cp_small:
         copy.wait()
@@ -314,78 +360,70 @@
         got(ids.at[src], id_r.at[d - 1], id_s.at[d - 1])
 
     def spread(j, carry):
-        column = jnp.broadcast_to(ids[j, 0:1, :], (B, B)).T
-        at = pl.ds(8 * j, 8)
-        high[at] = lax.shift_right_logical(column, 8).astype(F32).astype(BF16).reshape(8, 16, B)
-        low[at] = (column & (PLANE - 1)).astype(F32).astype(BF16).reshape(8, 16, B)
         line = jnp.broadcast_to(ids[j, 0:1, :], (16, B))
         high_row[j] = lax.shift_right_logical(line, 8).astype(F32).astype(BF16)
         low_row[j] = (line & (PLANE - 1)).astype(F32).astype(BF16)
-        gacc[j] = jnp.zeros((B, B), F32)
         return carry
 
     lax.fori_loop(0, 8, spread, 0)
 
+    for e in range(Y):
+        for d in range(CTX):
+            if e or d:
+                src = ctx_at(CTX - d)
+                got(wishes.at[e, src], w_r.at[e, src], w_s.at[0, 0])
+
+    def spread_wish(i, carry):
+        e, chip = lax.div(i, 4), lax.rem(i, 4)
+        line = wishes[e, 2 * chip, 0:1, :] + wishes[e, 2 * chip + 1, 0:1, :]
+        wish = jnp.broadcast_to(line, (B, B)).T.astype(I32) - 1
+        at = pl.ds(8 * i, 8)
+        high[at] = lax.shift_right_arithmetic(wish, 8).astype(F32).astype(BF16).reshape(8, 16, B)
+        low[at] = (wish & (PLANE - 1)).astype(F32).astype(BF16).reshape(8, 16, B)
+        return carry
+
+    lax.fori_loop(0, 16, spread_wish, 0)
+
     one, zero, none = jnp.asarray(1, BF16), jnp.asarray(0, BF16), jnp.asarray(-1, BF16)
-    lane = lax.broadcasted_iota(I32, (16, B), 1).astype(F32).astype(BF16)
-
-    def gather_tile(d, g):
-        this = jnp.asarray(d * GROUPS + g, BF16)
-        wanted = jnp.where(high[...] == this, low[...], none)
+    lane16 = lax.broadcasted_iota(I32, (16, B), 1).astype(F32).astype(BF16)
+
+    def pick(e, g):
+        at = slice(32 * e, 32 * (e + 1))
+        wanted = jnp.where(high[at] == jnp.asarray(g, BF16), low[at], none)
         hot = jnp.concatenate(
             [
-                jnp.where(wanted == (lane + jnp.asarray(k * B, BF16))[None], one, zero)
-                .reshape(8 * B, B)
+                jnp.where(wanted == (lane16 + jnp.asarray(k * B, BF16))[None], one, zero)
+                .reshape(4 * B, B)
                 for k in range(2)
             ],
             axis=1,
         )
-        rows = tbl[d, GROUPS * g : GROUPS * (g + 1)].reshape(PLANE, B)
-        gacc[...] = gacc[...] + dot(hot, rows).reshape(8, B, B)
-
-    slot_got(SLOT_OF[-LEAP])
-    for f in range(LEAP, 0, -1):
-        far_send(0, f).start()
-    slot_got(SLOT_OF[LEAP])
-    for f in range(LEAP, 0, -1):
-        far_send(1, f).start()
-
-    def pass_on(g):
+        rows = tbl[GROUPS * g : GROUPS * (g + 1)].reshape(PLANE, B)
+        return dot(hot, rows).reshape(4, B, B)
+
+    for g in range(GROUPS):
         for to in range(GROUPS * g, GROUPS * (g + 1)):
             if to and abs(SLOTS[to]) != LEAP:
                 slot_got(to)
-        for d in (2, 1, 3):
-            group_send(d, g).start()
-
-    pass_on(0)
-    pass_on(1)
-    gather_tile(0, 0)
-    gather_tile(0, 1)
-    for d in (1, 3, 2):
-        group_got(d, 0)
-        gather_tile(d, 0)
-    pass_on(2)
-    pass_on(3)
-    gather_tile(0, 2)
-    gather_tile(0, 3)
-    for g in (1, 2, 3):
-        for d in (1, 3, 2):
-            group_got(d, g)
-            gather_tile(d, g)
-
-    for j in range(8):
-        g1[j] = gacc[j].astype(BF16)
-    for d in FAR_FIRST:
-        dst = ctx_at(d)
-        remote(g1.at[dst], x1.at[c], a1_s.at[d - 1], a1_r.at[d - 1], dst, t).start()
-    x1[c] = g1[c]
-    for d in range(1, CTX):
-        src = ctx_at(CTX - d)
-        got(x1.at[src], a1_r.at[d - 1], a1_s.at[d - 1])
+        for e in (2, 1, 3, 0):
+            at = slice(4 * e, 4 * (e + 1))
+            found = pick(e, g) if g == 0 else gacc[at] + pick(e, g)
+            if g < GROUPS - 1:
+                gacc[at] = found
+            else:
+                picked[at] = found.astype(BF16)
+                for d in FAR_FIRST + ((0,) if e else ()):
+                    row_send(e, d).start()
+    here = pl.ds(pl.multiple_of(core * ASKED, ASKED), ASKED)
+    x1[c, pl.ds(pl.multiple_of(y * ASKED, ASKED), ASKED)] = picked[x, here]
+    for e in (0, 1, 3, 2):
+        for d in range(CTX):
+            if e or d:
+                row_got(e, ctx_at(CTX - d))
 
     total = jnp.zeros((B, B), F32)
     for j in range(8):
-        value = xin[j] + x1[j].astype(F32)
+        value = xin[j] + dot(unpack[...], x1[j])
         xin[j] = value
         total = total + value
     mean = jnp.sum(total, axis=1, keepdims=True) * (1.0 / MODEL)
@@ -563,13 +601,13 @@
             for b in range(0, SPLIT + REACH - 1) if s == 0 else range(SPLIT, 8):
                 send_back(atts, at_s, at_r.at[s, x], ratt.at[s, x], b)
 
-    sub = lax.broadcasted_iota(I32, (PLANE, B), 0).astype(F32).astype(BF16).reshape(16, 16, B)
+    sub16 = lax.broadcasted_iota(I32, (PLANE, B), 0).astype(F32).astype(BF16).reshape(16, 16, B)
 
     def tile_sum(d, g):
         this = jnp.asarray(d * GROUPS + g, BF16)
         wanted = jnp.where(high_row[...] == this, low_row[...], none)
         hot = jnp.concatenate(
-            [jnp.where(sub == wanted[j][None], one, zero).reshape(PLANE, B) for j in range(8)],
+            [jnp.where(sub16 == wanted[j][None], one, zero).reshape(PLANE, B) for j in range(8)],
             axis=1,
         )
         return dot(hot, gin[...].reshape(8 * B, B))
@@ -637,46 +675,23 @@
     drain()
 
 
-def adagrad(
-    grad_hbm, att_hbm, masters_hbm, accum_hbm, att_out, rg_out, nm_out, na_out,
-    grad, rows, accum, rg, nm, na, sem,
-):
-    copies = [
-        pltpu.make_async_copy(src, dst, sem.at[i])
-        for i, (src, dst) in enumerate(
-            ((grad_hbm, grad), (masters_hbm, rows), (accum_hbm, accum), (att_hbm, att_out))
-        )
-    ]
-    for copy in copies:
-        copy.start()
-    copies[0].wait()
+def adagrad(grad, att, rows, accum, att_out, rg_out, nm_out, na_out):
+    att_out[...] = att[...]
     total = jnp.zeros((ROWS, B), F32)
     for j in range(8):
         g = grad[j].astype(F32)
-        rg[:, j * B : (j + 1) * B] = g
+        rg_out[:, j * B : (j + 1) * B] = g
         total = total + g * g
-    results = [
-        pltpu.make_async_copy(src, dst, sem.at[4 + i])
-        for i, (src, dst) in enumerate(((rg, rg_out), (nm, nm_out), (na, na_out)))
-    ]
-    results[0].start()
-    copies[2].wait()
     diagonal = lax.broadcasted_iota(I32, (ROWS, ROWS), 0) == lax.broadcasted_iota(
         I32, (ROWS, ROWS), 1
     )
     before = jnp.sum(jnp.where(diagonal, accum[...], 0.0), axis=1, keepdims=True)
     after = before + jnp.sum(total, axis=1, keepdims=True) * (1.0 / MODEL)
     rate = LEARN_RATE * lax.rsqrt(after)
-    copies[1].wait()
     for j in range(8):
         cols = slice(j * B, (j + 1) * B)
-        nm[:, cols] = rows[:, cols] - rg[:, cols] * rate
-    results[1].start()
-    na[...] = jnp.sum(jnp.where(diagonal, after, 0.0), axis=0, keepdims=True)
-    results[2].start()
-    copies[3].wait()
-    for copy in results:
-        copy.wait()
+        nm_out[:, cols] = rows[:, cols] - grad[j].astype(F32) * rate
+    na_out[...] = jnp.sum(jnp.where(diagonal, after, 0.0), axis=0, keepdims=True)
 
 
 def per_device(
@@ -700,15 +715,18 @@
         pltpu.VMEM((B, HEADS * B), BF16),
         pltpu.VMEM((ROWS, B), F32),
         pltpu.VMEM((HEADS, MODEL, 3 * B), BF16),
-        block(Y, Z, rows=ROWS),
+        block(Z, rows=ROWS),
         block(8, rows=8, dtype=I32),
-        block(HEADS * 16, rows=16),
-        block(HEADS * 16, rows=16),
+        block(128, rows=16),
+        block(128, rows=16),
         block(8, rows=16),
         block(8, rows=16),
-        block(8, dtype=F32),
-        block(8),
-        block(8),
+        block(cols=2 * B),
+        block(Y, rows=8, dtype=F32),
+        block(Y, CTX, rows=8, dtype=F32),
+        block(16, dtype=F32),
+        block(16),
+        block(8, rows=Y * ASKED),
         block(8, dtype=F32),
         block(cols=MODEL),
         block(8, dtype=I32),
@@ -739,10 +757,10 @@
         block(2 * LEAP, rows=ROWS),
         block(8, rows=ROWS),
         dma((22,)),
-        dma((Y - 1, GROUPS)), dma((Y - 1, GROUPS)),
+        dma((Y, CTX)), dma((Y, CTX)),
         dma((Z + 1,)), dma((Z + 1,)),
         dma((7,)), dma((7,)),
-        dma((7,)), dma((7,)),
+        dma((Y, CTX)), dma((Y, CTX)),
         dma((HEADS, 2)), dma((8,)),
         dma((HEADS,)), dma((8,)),
         dma((HEADS, 2)), dma((8,)),
@@ -779,17 +797,8 @@
             jax.ShapeDtypeStruct((ROWS, MODEL), F32),
             jax.ShapeDtypeStruct((1, ROWS), F32),
         ),
-        in_specs=[hbm] * 4,
-        out_specs=(hbm, hbm, hbm, hbm),
-        scratch_shapes=[
-            block(8, rows=ROWS),
-            pltpu.VMEM((ROWS, MODEL), F32),
-            pltpu.VMEM((1, ROWS), F32),
-            pltpu.VMEM((ROWS, MODEL), F32),
-            pltpu.VMEM((ROWS, MODEL), F32),
-            pltpu.VMEM((1, ROWS), F32),
-            dma((7,)),
-        ],
+        in_specs=[vmem] * 4,
+        out_specs=(vmem, vmem, vmem, vmem),
         compiler_params=pltpu.CompilerParams(vmem_limit_bytes=VMEM_BYTES),
     )(grads, attended, masters, row_accum[None, :])
     return (attended[None], row_grads, new_masters, new_accum[0])

time: 94.7 us -> 85.7 us (0.905)
  Pallas kernels: 93.7 us -> 84.9 us
    pallas_call x1, Pallas kernels: 88.6 us -> 83 us  [per_device(): pl.pallas_call(kernel, out_shape=(jax.ShapeDtypeStruct((B, HEADS * B), BF...]
    pallas_call x1, Pallas kernels: 5.14 us -> 1.95 us  [per_device(): pl.pallas_call(adagrad, out_shape=(jax.ShapeDtypeStruct((B, HEADS * B), B...]
where the time goes in v4:
time: 85.7 us; the launch traced here: 85.6 us
  Pallas kernels  84.9 us (99%)
    pallas_call x1, Pallas kernels, per_device(): pl.pallas_call(kernel, out_shape=(jax.ShapeDtypeStruct((B, HEADS * B), BF...  83 us
    pallas_call x1, Pallas kernels, per_device(): pl.pallas_call(adagrad, out_shape=(jax.ShapeDtypeStruct((B, HEADS * B), B...  1.95 us

profile of v4, /device:TPU:1, one launch (start us, length us, event | category | flops | bytes accessed | tf_op | source)
XLA Modules:
  0.0 85.6 jit_solution(15481369781805179833)
XLA Ops:
  0.6 83.0 %shard_map.129 = (bf16[128,512]{1,0:T(8,128)(2,1)}, bf16[8,64,128]{2,1,0:T(8,128)(2,1)}) custom-call(s32[1,128]{1,0:T(1,128)} %bitcast.9, s32[1,128]{1,0:T(1,128)} %row_hbm.1, s32[1,128]{1,0:T(1,128)} %act_hbm.1, s32[1,4]{1,0:T(1,128)} %hist_hbm.1, f32[64,1024]{1,0:T(8,128)} %rows.1, f32[8,1024]{1,0:T(8,128)} %atab_hbm.1, f32[1,1024]{1,0:T(1,128)} %bitcast.7, ...), custom_call_target="tpu_custom_call" | custom-call | tf_op jit(solution)/shard_map/pallas_call | solution.py:776
  83.6 1.9 %shard_map.130 = (bf16[128,512]{1,0:T(8,128)(2,1)}, f32[64,1024]{1,0:T(8,128)}, f32[64,1024]{1,0:T(8,128)}, f32[1,64]{1,0:T(1,128)}) custom-call(bf16[8,64,128]{2,1,0:T(8,128)(2,1)} %get-tuple-element.10.grad, bf16[128,512]{1,0:T(8,128)(2,1)} %get-tuple-element.11.att, f32[64,1024]{1,0:T(8,128)} %rows.1, f32[1,64]{1,0:T(1,128)} %bitcast.8), custom_call_target="tpu_custom_call" | custom-call | tf_op jit(solution)/shard_map/pallas_call | solution.py:792

commit v5 on v4

--- a/solution.py
+++ b/solution.py
@@ -52,12 +52,12 @@
     dout_hbm,
     att_out, grad_out,
     owner_ref, row_ref, act_ref, hist_ref, atab_ref, gain_ref, dout_ref,
-    mslice, w_v, tbl, ids, high, low, high_row, low_row, unpack, wish_out, wishes,
+    mslice, w_v, tbl, high, low, high_row, low_row, unpack, pack, wish_out, wishes,
     gacc, picked, x1, xin, hn, startb, invb,
     pd, stq, stkv, qb, kvb, dob, attacc, dqacc, dqs, dkvs, atts, rdq, rdkv, ratt, dqf, gh,
-    g2, gin, psum, own, yb, stage, agg, zb, fin,
-    loc_s, w_s, w_r, z_s, z_r, id_s, id_r, a1_s, a1_r, q_s, q_r, kv_s, kv_r, do_s, do_r,
-    dq_s, dq_r, dkv_s, dkv_r, at_s, at_r, a2_s, a2_r, ry_s, ry_r, ag_s, ag_r, rz_s, rz_r, f_s, f_r,
+    g2, packed, gin, own, stage, agg, zb, fin,
+    loc_s, w_s, w_r, z_s, z_r, a1_s, a1_r, q_s, q_r, kv_s, kv_r, do_s, do_r,
+    dq_s, dq_r, dkv_s, dkv_r, at_s, at_r, a2_s, a2_r, ag_s, ag_r, rz_s, rz_r, f_s, f_r,
 ):
     c = lax.axis_index("ctx")
     t = lax.axis_index("tab")
@@ -92,6 +92,17 @@
         masters_ref.at[:, pl.ds(pl.multiple_of(c * B, B), B)], mslice, loc_s.at[0]
     )
     cp_slice.start()
+
+    barrier = pltpu.get_barrier_semaphore()
+    for d in range(LEAP, 0, -1):
+        for e in (d, -d):
+            pl.semaphore_signal(barrier, inc=1, device_id=(c, tab_z(e)), device_id_type=MESH)
+    for e in (2, 1, 3, 0):
+        for d in FAR_FIRST + ((0,) if e else ()):
+            pl.semaphore_signal(
+                barrier, inc=1, device_id=(ctx_at(d), tab_y(e)), device_id_type=MESH
+            )
+
     cp_ids = []
     for i, (src, dst) in enumerate(((owner_hbm, owner_ref), (row_hbm, row_ref))):
         cp_ids.append(pltpu.make_async_copy(src, dst, loc_s.at[14 + i]))
@@ -117,17 +128,6 @@
                 )
             )
 
-    barrier = pltpu.get_barrier_semaphore()
-    for d in range(1, LEAP + 1):
-        for e in (d, -d):
-            pl.semaphore_signal(barrier, inc=1, device_id=(c, tab_z(e)), device_id_type=MESH)
-    for e in range(Y):
-        for d in range(CTX):
-            if e or d:
-                pl.semaphore_signal(
-                    barrier, inc=1, device_id=(ctx_at(d), tab_y(e)), device_id_type=MESH
-                )
-
     cp_slice.wait()
     tbl[0] = mslice[...].astype(BF16)
     pl.semaphore_wait(barrier, Y * CTX - 1 + 2 * LEAP)
@@ -166,8 +166,6 @@
     slot = jnp.where(ahead > Z // 2, 2 * (Z - ahead), jnp.maximum(2 * ahead - 1, 0))
     asked = slot * ROWS + row
     owner_y = owner & (Y - 1)
-    behind = (y + Y - owner_y) & (Y - 1)
-    ids[c] = jnp.broadcast_to(behind * (Z * ROWS) + asked, (8, B))
 
     lane = lax.broadcasted_iota(I32, (B, B), 1)
     sub = lax.broadcasted_iota(I32, (B, B), 0)
@@ -179,6 +177,7 @@
     pos = column_y * ASKED + jnp.broadcast_to(rank, (B, B)).astype(I32)
     for k in range(2):
         unpack[:, k * B : (k + 1) * B] = jnp.where(pos == lane + k * B, 1.0, 0.0).astype(BF16)
+        pack[k * B : (k + 1) * B] = jnp.where(pos.T == sub + k * B, 1.0, 0.0).astype(BF16)
     number = lane - core * ASKED
     valid = (number >= 0) & (number < ASKED)
     for e in range(Y):
@@ -195,8 +194,6 @@
         for d in FAR_FIRST + ((0,) if e else ()):
             wish_send(e, d).start()
     wishes[0, c] = wish_out[0]
-    for d in FAR_FIRST:
-        remote(ids.at[c], ids.at[c], id_s.at[d - 1], id_r.at[d - 1], ctx_at(d), t).start()
 
     def row_send(e, d):
         to = ctx_at(d)
@@ -211,13 +208,18 @@
         at = pl.ds(pl.multiple_of(((y + Y - e) & (Y - 1)) * ASKED, ASKED), ASKED)
         got(x1.at[src, at], a1_r.at[e, src], a1_s.at[0, 0])
 
-    def sum_send(d, g):
+    def grad_send(e, d):
+        to = ctx_at(d)
+        at = pl.ds(pl.multiple_of(((y + Y - e) & (Y - 1)) * ASKED, ASKED), ASKED)
         return remote(
-            psum.at[d, g], yb.at[d - 1, g], ry_s.at[d - 1, g], ry_r.at[d - 1, g], c, tab_y(-d)
-        )
-
-    def sum_got(d, g):
-        got(yb.at[d - 1, g], ry_r.at[d - 1, g], ry_s.at[d - 1, g])
+            packed.at[to, at],
+            gin.at[e * 4 + x, pl.ds(pl.multiple_of(core * ASKED, ASKED), ASKED)],
+            a2_s.at[e, d], a2_r.at[e, c], to, tab_y(-e),
+        )
+
+    def grad_got(e, src):
+        at = pl.ds(pl.multiple_of(lax.rem(src, 2) * ASKED, ASKED), ASKED)
+        got(gin.at[e * 4 + lax.div(src, 2), at], a2_r.at[e, src], a2_s.at[0, 0])
 
     def gather_send(slot):
         distance = SLOTS[slot]
@@ -249,16 +251,8 @@
     holder = jnp.where(c >= SPLIT, 1, 0)
 
     def drain(upto=9):
-        for d in range(1, Y):
-            for g in range(GROUPS):
-                if upto >= 8:
-                    sum_send(d, g).wait_send()
-        for d in range(1, CTX):
-            sent(ids.at[c], id_s.at[d - 1], id_r.at[d - 1])
-            if upto >= 7:
-                sent(g2.at[0], a2_s.at[d - 1], a2_r.at[d - 1])
-            if upto >= 9:
-                sent(fin.at[c], f_s.at[d - 1], f_r.at[d - 1])
+        for d in range(1, CTX) if upto >= 9 else ():
+            sent(fin.at[c], f_s.at[d - 1], f_r.at[d - 1])
         for e in nearest:
             near_send(e).wait_send()
         for e in range(Y):
@@ -267,6 +261,8 @@
                     wish_send(e, d).wait_send()
                     if upto >= 3:
                         row_send(e, d).wait_send()
+                    if upto >= 7:
+                        grad_send(e, d).wait_send()
         for side in range(2):
             for f in range(1, LEAP + 1):
                 far_send(side, f).wait_send()
@@ -299,7 +295,8 @@
                     @pl.when((c != b) & (core == s))
                     def _():
                         sent(dqs.at[b], dq_s.at[b], dq_r.at[0, 0])
-                        sent(atts.at[b], at_s.at[b], at_r.at[0, 0])
+                        if upto >= 8:
+                            sent(atts.at[b], at_s.at[b], at_r.at[0, 0])
 
     def to_heads(src_of, dst, ssem, rsem, local):
         for r in (2, 1, 3, 0):
@@ -355,18 +352,6 @@
         return carry
 
     lax.fori_loop(0, 8, spans, 0)
-    for d in range(1, CTX):
-        src = ctx_at(CTX - d)
-        got(ids.at[src], id_r.at[d - 1], id_s.at[d - 1])
-
-    def spread(j, carry):
-        line = jnp.broadcast_to(ids[j, 0:1, :], (16, B))
-        high_row[j] = lax.shift_right_logical(line, 8).astype(F32).astype(BF16)
-        low_row[j] = (line & (PLANE - 1)).astype(F32).astype(BF16)
-        return carry
-
-    lax.fori_loop(0, 8, spread, 0)
-
     for e in range(Y):
         for d in range(CTX):
             if e or d:
@@ -380,6 +365,9 @@
         at = pl.ds(8 * i, 8)
         high[at] = lax.shift_right_arithmetic(wish, 8).astype(F32).astype(BF16).reshape(8, 16, B)
         low[at] = (wish & (PLANE - 1)).astype(F32).astype(BF16).reshape(8, 16, B)
+        line = jnp.broadcast_to(line, (16, B)).astype(I32) - 1
+        high_row[i] = lax.shift_right_arithmetic(line, 8).astype(F32).astype(BF16)
+        low_row[i] = (line & (PLANE - 1)).astype(F32).astype(BF16)
         return carry
 
     lax.fori_loop(0, 16, spread_wish, 0)
@@ -587,41 +575,27 @@
         g = gh[:, j * B : (j + 1) * B]
         g2[j] = (inv_std * (g - mean_g - xin[j] * mean_c)).astype(BF16)
 
-    for d in FAR_FIRST:
-        dst = ctx_at(d)
-        remote(g2.at[dst], gin.at[c], a2_s.at[d - 1], a2_r.at[d - 1], dst, t).start()
-    gin[c] = g2[c]
-    for d in range(1, CTX):
-        src = ctx_at(CTX - d)
-        got(gin.at[src], a2_r.at[d - 1], a2_s.at[d - 1])
-
-    for s in range(2):
-        @pl.when(core == s)
-        def _():
-            for b in range(0, SPLIT + REACH - 1) if s == 0 else range(SPLIT, 8):
-                send_back(atts, at_s, at_r.at[s, x], ratt.at[s, x], b)
+    for d in FAR_FIRST + (0,):
+        to = ctx_at(d)
+        packed[to] = dot(pack[...], g2[to]).astype(BF16)
+        for e in (2, 1, 3, 0):
+            if e or d:
+                grad_send(e, d).start()
+    gin[x, here] = packed[c, pl.ds(pl.multiple_of(y * ASKED, ASKED), ASKED)]
+    for e in (0, 1, 3, 2):
+        for d in range(CTX):
+            if e or d:
+                grad_got(e, ctx_at(CTX - d))
 
     sub16 = lax.broadcasted_iota(I32, (PLANE, B), 0).astype(F32).astype(BF16).reshape(16, 16, B)
 
-    def tile_sum(d, g):
-        this = jnp.asarray(d * GROUPS + g, BF16)
-        wanted = jnp.where(high_row[...] == this, low_row[...], none)
+    for g in (3, 2, 1, 0):
+        wanted = jnp.where(high_row[...] == jnp.asarray(g, BF16), low_row[...], none)
         hot = jnp.concatenate(
-            [jnp.where(sub16 == wanted[j][None], one, zero).reshape(PLANE, B) for j in range(8)],
+            [jnp.where(sub16 == wanted[j][None], one, zero).reshape(PLANE, B) for j in range(16)],
             axis=1,
         )
-        return dot(hot, gin[...].reshape(8 * B, B))
-
-    for g in (3, 2, 1, 0):
-        for d in (2, 1, 3):
-            psum[d, g] = tile_sum(d, g).astype(BF16)
-            sum_send(d, g).start()
-        own[g] = tile_sum(0, g)
-    for g in (3, 2, 1, 0):
-        value = own[g]
-        for d in (1, 3, 2):
-            sum_got(d, g)
-            value = value + yb[d - 1, g].astype(F32)
+        value = dot(hot, gin[...].reshape(16 * B, B))
         own[g] = value
         for i in range(GROUPS):
             slot = GROUPS * g + i
@@ -629,6 +603,13 @@
                 stage[slot] = value[i * ROWS : (i + 1) * ROWS].astype(BF16)
                 for copy in gather_send(slot) if slot > 2 * LEAP else [target_send(slot)]:
                     copy.start()
+
+    for s in range(2):
+        @pl.when(core == s)
+        def _():
+            for b in range(0, SPLIT + REACH - 1) if s == 0 else range(SPLIT, 8):
+                send_back(atts, at_s, at_r.at[s, x], ratt.at[s, x], b)
+
     for side in range(2):
         slot = SLOT_OF[LEAP if side == 0 else -LEAP]
         i = slot % GROUPS
@@ -716,12 +697,12 @@
         pltpu.VMEM((ROWS, B), F32),
         pltpu.VMEM((HEADS, MODEL, 3 * B), BF16),
         block(Z, rows=ROWS),
-        block(8, rows=8, dtype=I32),
         block(128, rows=16),
         block(128, rows=16),
-        block(8, rows=16),
-        block(8, rows=16),
+        block(16, rows=16),
+        block(16, rows=16),
         block(cols=2 * B),
+        block(rows=2 * B),
         block(Y, rows=8, dtype=F32),
         block(Y, CTX, rows=8, dtype=F32),
         block(16, dtype=F32),
@@ -748,10 +729,9 @@
         block(dtype=F32),
         block(cols=MODEL, dtype=F32),
         block(8),
-        block(8),
-        block(Y, GROUPS, rows=PLANE),
+        block(8, rows=Y * ASKED),
+        block(16),
         block(GROUPS, rows=PLANE, dtype=F32),
-        block(Y - 1, GROUPS, rows=PLANE),
         block(Z, rows=ROWS),
         block(2, LEAP, rows=ROWS),
         block(2 * LEAP, rows=ROWS),
@@ -759,7 +739,6 @@
         dma((22,)),
         dma((Y, CTX)), dma((Y, CTX)),
         dma((Z + 1,)), dma((Z + 1,)),
-        dma((7,)), dma((7,)),
         dma((Y, CTX)), dma((Y, CTX)),
         dma((HEADS, 2)), dma((8,)),
         dma((HEADS,)), dma((8,)),
@@ -767,8 +746,7 @@
         dma((8,)), dma((2, HEADS)),
         dma((8,)), dma((HEADS,)),
         dma((8,)), dma((2, HEADS)),
-        dma((7,)), dma((7,)),
-        dma((Y - 1, GROUPS)), dma((Y - 1, GROUPS)),
+        dma((Y, CTX)), dma((Y, CTX)),
         dma((2, LEAP)), dma((2, LEAP)),
         dma((2 * LEAP,)), dma((2 * LEAP,)),
         dma((7,)), dma((7,)),

time: 85.7 us -> 82.9 us (0.967)
  Pallas kernels: 84.9 us -> 82.1 us
    pallas_call x1, Pallas kernels: 83 us -> 80.2 us  [per_device(): pl.pallas_call(kernel, out_shape=(jax.ShapeDtypeStruct((B, HEADS * B), BF...]
where the time goes in v5:
time: 82.9 us; the launch traced here: 82.8 us
  Pallas kernels  82.1 us (99%)
    pallas_call x1, Pallas kernels, per_device(): pl.pallas_call(kernel, out_shape=(jax.ShapeDtypeStruct((B, HEADS * B), BF...  80.2 us
    pallas_call x1, Pallas kernels, per_device(): pl.pallas_call(adagrad, out_shape=(jax.ShapeDtypeStruct((B, HEADS * B), B...  1.95 us

profile of v5, /device:TPU:1, one launch (start us, length us, event | category | flops | bytes accessed | tf_op | source)
XLA Modules:
  0.0 82.8 jit_solution(10388421057845155369)
XLA Ops:
  0.6 80.2 %shard_map.129 = (bf16[128,512]{1,0:T(8,128)(2,1)}, bf16[8,64,128]{2,1,0:T(8,128)(2,1)}) custom-call(s32[1,128]{1,0:T(1,128)} %bitcast.9, s32[1,128]{1,0:T(1,128)} %row_hbm.1, s32[1,128]{1,0:T(1,128)} %act_hbm.1, s32[1,4]{1,0:T(1,128)} %hist_hbm.1, f32[64,1024]{1,0:T(8,128)} %rows.1, f32[8,1024]{1,0:T(8,128)} %atab_hbm.1, f32[1,1024]{1,0:T(1,128)} %bitcast.7, ...), custom_call_target="tpu_custom_call" | custom-call | tf_op jit(solution)/shard_map/pallas_call | solution.py:754
  80.8 1.9 %shard_map.130 = (bf16[128,512]{1,0:T(8,128)(2,1)}, f32[64,1024]{1,0:T(8,128)}, f32[64,1024]{1,0:T(8,128)}, f32[1,64]{1,0:T(1,128)}) custom-call(bf16[8,64,128]{2,1,0:T(8,128)(2,1)} %get-tuple-element.10.grad, bf16[128,512]{1,0:T(8,128)(2,1)} %get-tuple-element.11.att, f32[64,1024]{1,0:T(8,128)} %rows.1, f32[1,64]{1,0:T(1,128)} %bitcast.8), custom_call_target="tpu_custom_call" | custom-call | tf_op jit(solution)/shard_map/pallas_call | solution.py:770

commit v6 on v5

--- a/solution.py
+++ b/solution.py
@@ -54,9 +54,9 @@
     owner_ref, row_ref, act_ref, hist_ref, atab_ref, gain_ref, dout_ref,
     mslice, w_v, tbl, high, low, high_row, low_row, unpack, pack, wish_out, wishes,
     gacc, picked, x1, xin, hn, startb, invb,
-    pd, stq, stkv, qb, kvb, dob, attacc, dqacc, dqs, dkvs, atts, rdq, rdkv, ratt, dqf, gh,
+    pd, sqkv, qkv, qf, dob, dkvacc, attacc, dqacc, dqs, dkvs, atts, rdq, rdkv, ratt, dqf, gh,
     g2, packed, gin, own, stage, agg, zb, fin,
-    loc_s, w_s, w_r, z_s, z_r, a1_s, a1_r, q_s, q_r, kv_s, kv_r, do_s, do_r,
+    loc_s, w_s, w_r, z_s, z_r, a1_s, a1_r, qkv_s, qkv_r, qf_s, qf_r, do_s, do_r,
     dq_s, dq_r, dkv_s, dkv_r, at_s, at_r, a2_s, a2_r, ag_s, ag_r, rz_s, rz_r, f_s, f_r,
 ):
     c = lax.axis_index("ctx")
@@ -276,13 +276,16 @@
                 @pl.when(need & (2 * h + s != c))
                 def _():
                     sent(dob.at[0], do_s.at[h, s], do_r.at[0])
-                    if upto >= 4:
-                        sent(stq.at[h], q_s.at[h, s], q_r.at[0])
 
             if upto >= 4:
                 @pl.when(2 * h + holder != c)
                 def _():
-                    sent(stkv.at[h], kv_s.at[h], kv_r.at[0])
+                    sent(sqkv.at[h], qkv_s.at[h], qkv_r.at[0])
+
+        for b in range(SPLIT, SPLIT + REACH - 1) if upto >= 5 else ():
+            @pl.when((core == 1) & (c != b + 1))
+            def _():
+                sent(qf.at[b], qf_s.at[b], qf_r.at[0])
 
         for b in range(8) if upto >= 5 else ():
             @pl.when((c != b) & (core == (0 if b < SPLIT else 1)))
@@ -427,41 +430,28 @@
     for copy in cp_w:
         copy.wait()
 
-    def q_of(h):
-        return stq.at[h]
-
-    def q_here(h):
-        qb[c] = stq[h]
-
     for r in (2, 1, 3, 0):
         h = lax.rem(x + r, HEADS)
         project = dot(hn[...], w_v[h])
         sig = sigmoid(project)
         pd[h] = sig * (1.0 + project * (1.0 - sig))
         active = (project * sig).astype(BF16)
-        stq[h] = active[:, 0:B]
-        stkv[h] = active[:, B : 3 * B]
+        sqkv[h] = active
         dev = 2 * h + holder
 
         @pl.when(dev != c)
         def _():
-            remote(stkv.at[h], kvb.at[c], kv_s.at[h], kv_r.at[c], dev, t).start()
+            remote(sqkv.at[h], qkv.at[c], qkv_s.at[h], qkv_r.at[c], dev, t).start()
 
         @pl.when(dev == c)
         def _():
-            kvb[c] = stkv[h]
-
-        for s in (1, 0):
-            need = (c <= SPLIT + REACH - 2) if s == 0 else (c >= SPLIT)
-            to = 2 * h + s
-
-            @pl.when(need & (to != c))
-            def _():
-                remote(stq.at[h], qb.at[c], q_s.at[h, s], q_r.at[c], to, t).start()
-
-            @pl.when(need & (to == c))
-            def _():
-                q_here(h)
+            qkv[c] = sqkv[h]
+
+    both = (c >= SPLIT) & (c <= SPLIT + REACH - 2)
+
+    @pl.when(both & (core == 0))
+    def _():
+        qf[c] = sqkv[x, :, 0:B]
 
     def send_back(ready, ssem, rsem, dst, block):
         @pl.when(c != block)
@@ -472,66 +462,93 @@
         def _():
             dst[...] = ready[block]
 
-    def attend(s):
-        key_blocks = range(0, SPLIT) if s == 0 else range(SPLIT, 8)
-        lowest = key_blocks[0]
-        waited = set()
-        for kb in key_blocks:
+    def block_got(b):
+        @pl.when(c != b)
+        def _():
+            got(qkv.at[b], qkv_r.at[b], qkv_s.at[0])
+            got(dob.at[b], do_r.at[b], do_s.at[0, 0])
+
+    def tile(kb, low_q, end_q, queries):
+        n = (end_q - low_q) * B
+        queries = queries.reshape(n, B)
+        cotangent = dob[low_q:end_q].reshape(n, B)
+        keys = qkv[kb, :, B : 2 * B]
+        values = qkv[kb, :, 2 * B : 3 * B]
+        raw = dot(queries, keys, NT) * SCALE
+        sig = sigmoid(raw)
+        inv = invb[low_q:end_q].reshape(n, B)
+        k_pos = lax.broadcasted_iota(I32, (n, B), 1) + kb * B
+        q_pos = lax.broadcasted_iota(I32, (n, B), 0) + low_q * B
+        allowed = (k_pos >= startb[low_q:end_q].reshape(n, B)) & (k_pos <= q_pos)
+        weights = jnp.where(allowed, raw * sig * inv, 0.0).astype(BF16)
+        grad_w = dot(cotangent, values, NT)
+        slope = sig * (1.0 + raw * (1.0 - sig))
+        grad_raw = jnp.where(allowed, grad_w * slope * (inv * SCALE), 0.0).astype(BF16)
+        dkv = jnp.concatenate([dot(grad_raw, queries, TN), dot(weights, cotangent, TN)], axis=1)
+        return dkv, dot(grad_raw, keys), dot(weights, values)
+
+    def keep(s, kb, low_q, end_q, dq, at):
+        lowest, highest = (0, SPLIT - 1) if s == 0 else (SPLIT, 7)
+        for b in range(low_q, end_q):
+            rows = slice((b - low_q) * B, (b - low_q + 1) * B)
+            first = kb == max(b - REACH + 1, lowest)
+            dq_b = dq[rows] if first else dqacc[b] + dq[rows]
+            at_b = at[rows] if first else attacc[b] + at[rows]
+            if kb == min(b, highest):
+                dqs[b] = dq_b.astype(BF16)
+                send_back(dqs, dq_s, dq_r.at[s, x], rdq.at[s, x], b)
+                atts[b] = at_b.astype(BF16)
+            else:
+                dqacc[b] = dq_b
+                attacc[b] = at_b
+
+    def dkv_back(kb, dkv):
+        dkvs[kb] = dkv.astype(BF16)
+        send_back(dkvs, dkv_s, dkv_r.at[x], rdkv.at[x], kb)
+
+    def hand_on(b):
+        return remote(
+            qkv.at[b, :, pl.ds(0, B)], qf.at[b], qf_s.at[b], qf_r.at[b], 2 * x, t
+        )
+
+    shared = range(SPLIT, SPLIT + REACH - 1)
+
+    @pl.when(core == 0)
+    def _():
+        for b in range(SPLIT):
+            block_got(b)
+        for kb in range(SPLIT):
+            dkv, dq, at = tile(kb, kb, SPLIT, qkv[kb:SPLIT, :, 0:B])
+            dkvacc[kb] = dkv
+            keep(0, kb, kb, SPLIT, dq, at)
+        for b in shared:
+            @pl.when(c != b)
+            def _():
+                got(qf.at[b], qf_r.at[b], qf_s.at[0])
+                got(dob.at[b], do_r.at[b], do_s.at[0, 0])
+
+        for kb in range(SPLIT):
+            dkv, dq, at = tile(kb, SPLIT, kb + REACH, qf[SPLIT : kb + REACH])
+            dkv_back(kb, dkvacc[kb] + dkv)
+            keep(0, kb, SPLIT, kb + REACH, dq, at)
+
+    @pl.when(core == 1)
+    def _():
+        for b in shared:
+            block_got(b)
+
+            @pl.when(c != b + 1)
+            def _():
+                hand_on(b).start()
+
+        for b in range(SPLIT + REACH - 1, 8):
+            block_got(b)
+        for kb in range(SPLIT, 8):
             end = min(kb + REACH, 8)
-            n = (end - kb) * B
-
-            @pl.when(c != kb)
-            def _():
-                got(kvb.at[kb], kv_r.at[kb], kv_s.at[0])
-
-            for b in range(kb, end):
-                if b not in waited:
-                    waited.add(b)
-
-                    @pl.when(c != b)
-                    def _():
-                        got(qb.at[b], q_r.at[b], q_s.at[0, 0])
-                        got(dob.at[b], do_r.at[b], do_s.at[0, 0])
-
-            queries = qb[kb:end].reshape(n, B)
-            cotangent = dob[kb:end].reshape(n, B)
-            keys = kvb[kb, :, 0:B]
-            values = kvb[kb, :, B : 2 * B]
-            raw = dot(queries, keys, NT) * SCALE
-            sig = sigmoid(raw)
-            inv = invb[kb:end].reshape(n, B)
-            k_pos = lax.broadcasted_iota(I32, (n, B), 1) + kb * B
-            q_pos = lax.broadcasted_iota(I32, (n, B), 0) + kb * B
-            allowed = (k_pos >= startb[kb:end].reshape(n, B)) & (k_pos <= q_pos)
-            weights = jnp.where(allowed, raw * sig * inv, 0.0).astype(BF16)
-            grad_w = dot(cotangent, values, NT)
-            slope = sig * (1.0 + raw * (1.0 - sig))
-            grad_raw = jnp.where(allowed, grad_w * slope * (inv * SCALE), 0.0).astype(BF16)
-            dkvs[kb, :, 0:B] = dot(grad_raw, queries, TN).astype(BF16)
-            dkvs[kb, :, B : 2 * B] = dot(weights, cotangent, TN).astype(BF16)
-            send_back(dkvs, dkv_s, dkv_r.at[x], rdkv.at[x], kb)
-            dq = dot(grad_raw, keys)
-            at = dot(weights, values)
-            for b in range(kb, end):
-                rows = slice((b - kb) * B, (b - kb + 1) * B)
-                first = kb == max(b - REACH + 1, lowest)
-                last = kb == min(b, key_blocks[-1])
-                dq_b = dq[rows] if first else dqacc[b] + dq[rows]
-                at_b = at[rows] if first else attacc[b] + at[rows]
-                if last:
-                    dqs[b] = dq_b.astype(BF16)
-                    send_back(dqs, dq_s, dq_r.at[s, x], rdq.at[s, x], b)
-                    atts[b] = at_b.astype(BF16)
-                else:
-                    dqacc[b] = dq_b
-                    attacc[b] = at_b
-
-    for s in range(2):
-        @pl.when(core == s)
-        def _():
-            attend(s)
-
-    both = (c >= SPLIT) & (c <= SPLIT + REACH - 2)
+            dkv, dq, at = tile(kb, kb, end, qkv[kb:end, :, 0:B])
+            dkv_back(kb, dkv)
+            keep(1, kb, kb, end, dq, at)
+
     for r in (0, 1, 3, 2):
         h = lax.rem(x + r, HEADS)
 
@@ -713,11 +730,11 @@
         block(8, dtype=I32),
         block(8, dtype=F32),
         block(HEADS, cols=3 * B, dtype=F32),
-        block(HEADS),
-        block(HEADS, cols=2 * B),
+        block(HEADS, cols=3 * B),
+        block(8, cols=3 * B),
         block(8),
-        block(8, cols=2 * B),
         block(8),
+        block(SPLIT, cols=2 * B, dtype=F32),
         block(8, dtype=F32),
         block(8, dtype=F32),
         block(8),
@@ -740,8 +757,8 @@
         dma((Y, CTX)), dma((Y, CTX)),
         dma((Z + 1,)), dma((Z + 1,)),
         dma((Y, CTX)), dma((Y, CTX)),
-        dma((HEADS, 2)), dma((8,)),
         dma((HEADS,)), dma((8,)),
+        dma((8,)), dma((8,)),
         dma((HEADS, 2)), dma((8,)),
         dma((8,)), dma((2, HEADS)),
         dma((8,)), dma((HEADS,)),

time: 82.9 us -> 81.4 us (0.982)
  Pallas kernels: 82.1 us -> 80.6 us
    pallas_call x1, Pallas kernels: 80.2 us -> 78.7 us  [per_device(): pl.pallas_call(kernel, out_shape=(jax.ShapeDtypeStruct((B, HEADS * B), BF...]
where the time goes in v6:
time: 81.4 us; the launch traced here: 81.3 us
  Pallas kernels  80.6 us (99%)
    pallas_call x1, Pallas kernels, per_device(): pl.pallas_call(kernel, out_shape=(jax.ShapeDtypeStruct((B, HEADS * B), BF...  78.7 us
    pallas_call x1, Pallas kernels, per_device(): pl.pallas_call(adagrad, out_shape=(jax.ShapeDtypeStruct((B, HEADS * B), B...  1.95 us

profile of v6, /device:TPU:1, one launch (start us, length us, event | category | flops | bytes accessed | tf_op | source)
XLA Modules:
  0.0 81.3 jit_solution(15928026618446985321)
XLA Ops:
  0.6 78.7 %shard_map.129 = (bf16[128,512]{1,0:T(8,128)(2,1)}, bf16[8,64,128]{2,1,0:T(8,128)(2,1)}) custom-call(s32[1,128]{1,0:T(1,128)} %bitcast.9, s32[1,128]{1,0:T(1,128)} %row_hbm.1, s32[1,128]{1,0:T(1,128)} %act_hbm.1, s32[1,4]{1,0:T(1,128)} %hist_hbm.1, f32[64,1024]{1,0:T(8,128)} %rows.1, f32[8,1024]{1,0:T(8,128)} %atab_hbm.1, f32[1,1024]{1,0:T(1,128)} %bitcast.7, ...), custom_call_target="tpu_custom_call" | custom-call | tf_op jit(solution)/shard_map/pallas_call | solution.py:771
  79.3 1.9 %shard_map.130 = (bf16[128,512]{1,0:T(8,128)(2,1)}, f32[64,1024]{1,0:T(8,128)}, f32[64,1024]{1,0:T(8,128)}, f32[1,64]{1,0:T(1,128)}) custom-call(bf16[8,64,128]{2,1,0:T(8,128)(2,1)} %get-tuple-element.10.grad, bf16[128,512]{1,0:T(8,128)(2,1)} %get-tuple-element.11.att, f32[64,1024]{1,0:T(8,128)} %rows.1, f32[1,64]{1,0:T(1,128)} %bitcast.8), custom_call_target="tpu_custom_call" | custom-call | tf_op jit(solution)/shard_map/pallas_call | solution.py:787

commit v7 on v6

--- a/solution.py
+++ b/solution.py
@@ -157,7 +157,7 @@
                 got(tbl.at[15, half_rows[side]], z_r.at[15 + side], z_s.at[15 + side])
 
     nearest = [e for d in range(LEAP, 0, -1) for e in (d, -d)]
-    for e in nearest:
+    for e in nearest[:2]:
         near_send(e).start()
     for copy in cp_ids:
         copy.wait()
@@ -190,6 +190,8 @@
             wish_out.at[e], wishes.at[e, c], w_s.at[e, d], w_r.at[e, c], ctx_at(d), tab_y(-e)
         )
 
+    for e in nearest[2:]:
+        near_send(e).start()
     for e in (2, 1, 3, 0):
         for d in FAR_FIRST + ((0,) if e else ()):
             wish_send(e, d).start()
@@ -618,7 +620,7 @@
             slot = GROUPS * g + i
             if slot and abs(SLOTS[slot]) != LEAP:
                 stage[slot] = value[i * ROWS : (i + 1) * ROWS].astype(BF16)
-                for copy in gather_send(slot) if slot > 2 * LEAP else [target_send(slot)]:
+                for copy in gather_send(slot) if slot > 2 * LEAP else ():
                     copy.start()
 
     for s in range(2):
@@ -627,12 +629,17 @@
             for b in range(0, SPLIT + REACH - 1) if s == 0 else range(SPLIT, 8):
                 send_back(atts, at_s, at_r.at[s, x], ratt.at[s, x], b)
 
+    for side in range(2):
+        gather_got(side, 1)
+    for slot in range(2 * (LEAP - 1), 0, -1):
+        target_send(slot).start()
     for side in range(2):
         slot = SLOT_OF[LEAP if side == 0 else -LEAP]
         i = slot % GROUPS
         total = own[slot // GROUPS, i * ROWS : (i + 1) * ROWS, :]
         for f in range(1, LEAP):
-            gather_got(side, f)
+            if f > 1:
+                gather_got(side, f)
             total = total + agg[side, f - 1].astype(F32)
         gather_got(side, LEAP)
         stage[slot] = total.astype(BF16)

time: 81.4 us -> 82.1 us (level)
  no operation moved by 1% of the time
where the time goes in v7:
time: 82.1 us; the launch traced here: 81.9 us
  Pallas kernels  81.3 us (99%)
    pallas_call x1, Pallas kernels, per_device(): pl.pallas_call(kernel, out_shape=(jax.ShapeDtypeStruct((B, HEADS * B), BF...  79.3 us
    pallas_call x1, Pallas kernels, per_device(): pl.pallas_call(adagrad, out_shape=(jax.ShapeDtypeStruct((B, HEADS * B), B...  1.95 us

profile of v7, /device:TPU:1, one launch (start us, length us, event | category | flops | bytes accessed | tf_op | source)
XLA Modules:
  0.0 81.9 jit_solution(17410542381211886134)
XLA Ops:
  0.6 79.3 %shard_map.129 = (bf16[128,512]{1,0:T(8,128)(2,1)}, bf16[8,64,128]{2,1,0:T(8,128)(2,1)}) custom-call(s32[1,128]{1,0:T(1,128)} %bitcast.9, s32[1,128]{1,0:T(1,128)} %row_hbm.1, s32[1,128]{1,0:T(1,128)} %act_hbm.1, s32[1,4]{1,0:T(1,128)} %hist_hbm.1, f32[64,1024]{1,0:T(8,128)} %rows.1, f32[8,1024]{1,0:T(8,128)} %atab_hbm.1, f32[1,1024]{1,0:T(1,128)} %bitcast.7, ...), custom_call_target="tpu_custom_call" | custom-call | tf_op jit(solution)/shard_map/pallas_call | solution.py:778
  80.0 1.9 %shard_map.130 = (bf16[128,512]{1,0:T(8,128)(2,1)}, f32[64,1024]{1,0:T(8,128)}, f32[64,1024]{1,0:T(8,128)}, f32[1,64]{1,0:T(1,128)}) custom-call(bf16[8,64,128]{2,1,0:T(8,128)(2,1)} %get-tuple-element.10.grad, bf16[128,512]{1,0:T(8,128)(2,1)} %get-tuple-element.11.att, f32[64,1024]{1,0:T(8,128)} %rows.1, f32[1,64]{1,0:T(1,128)} %bitcast.8), custom_call_target="tpu_custom_call" | custom-call | tf_op jit(solution)/shard_map/pallas_call | solution.py:794

commit v8 on v6

--- a/solution.py
+++ b/solution.py
@@ -157,7 +157,7 @@
                 got(tbl.at[15, half_rows[side]], z_r.at[15 + side], z_s.at[15 + side])
 
     nearest = [e for d in range(LEAP, 0, -1) for e in (d, -d)]
-    for e in nearest:
+    for e in nearest[:2]:
         near_send(e).start()
     for copy in cp_ids:
         copy.wait()
@@ -190,6 +190,8 @@
             wish_out.at[e], wishes.at[e, c], w_s.at[e, d], w_r.at[e, c], ctx_at(d), tab_y(-e)
         )
 
+    for e in nearest[2:]:
+        near_send(e).start()
     for e in (2, 1, 3, 0):
         for d in FAR_FIRST + ((0,) if e else ()):
             wish_send(e, d).start()
@@ -621,12 +623,6 @@
                 for copy in gather_send(slot) if slot > 2 * LEAP else [target_send(slot)]:
                     copy.start()
 
-    for s in range(2):
-        @pl.when(core == s)
-        def _():
-            for b in range(0, SPLIT + REACH - 1) if s == 0 else range(SPLIT, 8):
-                send_back(atts, at_s, at_r.at[s, x], ratt.at[s, x], b)
-
     for side in range(2):
         slot = SLOT_OF[LEAP if side == 0 else -LEAP]
         i = slot % GROUPS
@@ -639,6 +635,12 @@
         at = slice(side * HALF, (side + 1) * HALF)
         stage[slot, at, :] = (total[at] + agg[side, LEAP - 1, at, :].astype(F32)).astype(BF16)
         target_send(slot).start()
+
+    for s in range(2):
+        @pl.when(core == s)
+        def _():
+            for b in range(0, SPLIT + REACH - 1) if s == 0 else range(SPLIT, 8):
+                send_back(atts, at_s, at_r.at[s, x], ratt.at[s, x], b)
 
     for h in range(HEADS):
         @pl.when(2 * h + holder != c)

time: 81.4 us -> 81.6 us (level)
  no operation moved by 1% of the time
where the time goes in v8:
time: 81.6 us; the launch traced here: 81.4 us
  Pallas kernels  80.8 us (99%)
    pallas_call x1, Pallas kernels, per_device(): pl.pallas_call(kernel, out_shape=(jax.ShapeDtypeStruct((B, HEADS * B), BF...  78.8 us
    pallas_call x1, Pallas kernels, per_device(): pl.pallas_call(adagrad, out_shape=(jax.ShapeDtypeStruct((B, HEADS * B), B...  1.95 us

profile of v8, /device:TPU:1, one launch (start us, length us, event | category | flops | bytes accessed | tf_op | source)
XLA Modules:
  0.0 81.4 jit_solution(10027131228425430962)
XLA Ops:
  0.6 78.8 %shard_map.129 = (bf16[128,512]{1,0:T(8,128)(2,1)}, bf16[8,64,128]{2,1,0:T(8,128)(2,1)}) custom-call(s32[1,128]{1,0:T(1,128)} %bitcast.9, s32[1,128]{1,0:T(1,128)} %row_hbm.1, s32[1,128]{1,0:T(1,128)} %act_hbm.1, s32[1,4]{1,0:T(1,128)} %hist_hbm.1, f32[64,1024]{1,0:T(8,128)} %rows.1, f32[8,1024]{1,0:T(8,128)} %atab_hbm.1, f32[1,1024]{1,0:T(1,128)} %bitcast.7, ...), custom_call_target="tpu_custom_call" | custom-call | tf_op jit(solution)/shard_map/pallas_call | solution.py:773
  79.5 1.9 %shard_map.130 = (bf16[128,512]{1,0:T(8,128)(2,1)}, f32[64,1024]{1,0:T(8,128)}, f32[64,1024]{1,0:T(8,128)}, f32[1,64]{1,0:T(1,128)}) custom-call(bf16[8,64,128]{2,1,0:T(8,128)(2,1)} %get-tuple-element.10.grad, bf16[128,512]{1,0:T(8,128)(2,1)} %get-tuple-element.11.att, f32[64,1024]{1,0:T(8,128)} %rows.1, f32[1,64]{1,0:T(1,128)} %bitcast.8), custom_call_target="tpu_custom_call" | custom-call | tf_op jit(solution)/shard_map/pallas_call | solution.py:789
